TPU v7x, 256 devices: a whole 4x4x8 slice. The times are simulated.
256 devices in a mesh: tm: 64 (over x, z, y_lo), sx: 2 (over core), sy: 2 (over y_hi).
Axes of the slice: x: 4, y: 4 (y_hi: 2, y_lo: 2; y = y_hi * 2 + y_lo), z: 8, core: 2. Of those that a mesh axis runs over, the one named last changes fastest.
Arguments:
- initial_states: float32 [64, 8, 64, 256], P('tm', None, 'sx', 'sy'), may hold values from -6 to 6
- coarse_decay: float32 [64, 8, 64, 256], P('tm', None, 'sx', 'sy'), may hold values from 0 to 1, as said below
- power_map: float32 [8, 64, 256], P(None, 'sx', 'sy'), may hold values from 0.5 to 2
- power_mask: int32 [64, 4, 8], P('tm'), may hold values 0 or 1
- region_ids: int32 [8, 8], replicated, may hold values from 0 to 3
- region_conductivity: float32 [4], replicated, may hold values from 0.4 to 2.5
Outputs:
- cycle_states: float32 [64, 8, 64, 256], P('tm', None, 'sx', 'sy')
- jump_field: float32 [64, 8, 64, 256], P('tm', None, 'sx', 'sy')
Inputs may be any that keep to these rules, and one draw needn't show every extreme that they name: `coarse_decay`: every entry lies between 0 and 1, and for every cell the product of its 64 factors is at most one half.
All inputs are finite; a program needn't handle non-finite values. No bound on the sum of `power_mask` on one device may be relied on, other than what follows from the above.
Results may differ from a plain program's by a relative error of at most 0.0001.
Values sent between devices are 32-bit elements; how exact they have to be, the bound alone decides.
No kernel may reach another device: no remote copies, remote signals or barrier semaphores. Data moves between devices by JAX's collectives and lax.ppermute only.
A program may use at most 128 MiB of HBM per device.

v0:
```python
import jax
import jax.numpy as jnp
from jax import lax
from jax.sharding import PartitionSpec as P

RB = 8
REGIONS = 4
FSTEPS = 4
SWEEPS = 3
ITERS = 2


grid_xy = 1.0
grid_z = 0.5
sink_gain = 0.5
source_gain = 0.5
cond_slope = 0.25
joule_slope = 0.3


def padded_2(x, sides, width):
    for axis, dim in sides:
        peers, length = (lax.axis_size(axis), x.shape[dim])
        up = [(i, (i + 1) % peers) for i in range(peers - 1)]
        down = [(j, i) for i, j in up]
        last = lax.slice_in_dim(x, length - width, length, axis=dim)
        initial = lax.slice_in_dim(x, 0, width, axis=dim)
        before = lax.ppermute(last, axis, up)
        after = lax.ppermute(initial, axis, down)
        x = jnp.concatenate([before, x, after], axis=dim)
    return x


def entering(x, axis, combine, identity):
    peers, here = (lax.axis_size(axis), lax.axis_index(axis))
    everything = jax.tree.map(lambda part: lax.all_gather(part, axis), x)
    start = jax.tree.map(
        lambda part, zero: jnp.broadcast_to(jnp.asarray(zero, part.dtype), part.shape), x, identity
    )

    def step(k, before):
        reached = k < here
        new = combine(before, jax.tree.map(lambda part: part[k], everything))
        return jax.tree.map(lambda a, b: jnp.where(reached, a, b), new, before)

    return lax.fori_loop(0, peers, step, start)


def broadcast(x, axis, root):
    mine = lax.axis_index(axis) == root
    return lax.psum(jnp.where(mine, x, jnp.zeros_like(x)), axis)


def passed_along(block, axis, distance):
    devices = range(lax.axis_size(axis))
    route = [((i - distance) % len(devices), i) for i in devices]
    return lax.ppermute(block, axis, route)


def base_rows(region_ids, region_conductivity):
    labels = jnp.arange(REGIONS, dtype=jnp.int32)
    chosen = (region_ids[:, :, None] == labels[None, None, :]).astype(jnp.float32)
    return jnp.sum(chosen * region_conductivity[None, None, :], axis=2)


def face_weights(cond_pad, weight_scale):
    middle = cond_pad[:, 1:-1, 1:-1]
    layer_index = lax.broadcasted_iota(jnp.int32, middle.shape, 0)
    blank_layer = jnp.zeros_like(middle[:1])
    layer_above = jnp.concatenate([middle[1:], blank_layer], axis=0)
    layer_below = jnp.concatenate([blank_layer, middle[:-1]], axis=0)
    weight_west = weight_scale * (grid_xy * (0.5 * (middle + cond_pad[:, :-2, 1:-1])))
    weight_east = weight_scale * (grid_xy * (0.5 * (middle + cond_pad[:, 2:, 1:-1])))
    weight_south = weight_scale * (grid_xy * (0.5 * (middle + cond_pad[:, 1:-1, :-2])))
    weight_north = weight_scale * (grid_xy * (0.5 * (middle + cond_pad[:, 1:-1, 2:])))
    weight_up = jnp.where(
        layer_index == middle.shape[0] - 1,
        jnp.zeros_like(middle),
        weight_scale * (grid_z * (0.5 * (middle + layer_above))),
    )
    weight_down = jnp.where(
        layer_index == 0,
        weight_scale * (sink_gain * middle),
        weight_scale * (grid_z * (0.5 * (middle + layer_below))),
    )
    denominator = 1.0 + (
        weight_west + weight_east + weight_south + weight_north + weight_down + weight_up
    )
    return (
        (weight_west, weight_east, weight_south, weight_north, weight_down, weight_up),
        denominator,
    )


def relax(padded, weights, right_side, denominator):
    weight_west, weight_east, weight_south, weight_north, weight_down, weight_up = weights
    middle = padded[:, 1:-1, 1:-1]
    blank_layer = jnp.zeros_like(middle[:1])
    layer_above = jnp.concatenate([middle[1:], blank_layer], axis=0)
    layer_below = jnp.concatenate([blank_layer, middle[:-1]], axis=0)
    summed = weight_west * padded[:, :-2, 1:-1] + weight_east * padded[:, 2:, 1:-1]
    summed = summed + weight_south * padded[:, 1:-1, :-2] + weight_north * padded[:, 1:-1, 2:]
    summed = summed + weight_down * layer_below + weight_up * layer_above
    return (right_side + summed) / denominator


def compose_forward(earlier, later):
    return (earlier[0] * later[0], later[0] * earlier[1] + later[1])


def shards(initial_states, coarse_decay, power_map, power_mask, region_ids, region_conductivity):
    tile_rows = initial_states.shape[2]
    tile_cols = initial_states.shape[3]
    block_count = region_ids.shape[1]
    row_first = lax.axis_index("sx") * tile_rows
    col_first = lax.axis_index("sy") * tile_cols
    grid_rows = tile_rows * lax.axis_size("sx")
    grid_cols = tile_cols * lax.axis_size("sy")
    per_block = base_rows(region_ids, region_conductivity)
    mask_blocks = power_mask[0].astype(jnp.float32)
    row_ids = row_first - 1 + jnp.arange(tile_rows + 2 * 1, dtype=jnp.int32)
    col_ids = col_first - 1 + jnp.arange(tile_cols + 2 * 1, dtype=jnp.int32)
    row_inside = ((row_ids >= 0) & (row_ids < grid_rows)).astype(jnp.float32)
    col_inside = ((col_ids >= 0) & (col_ids < grid_cols)).astype(jnp.float32)
    block_of = jnp.clip(row_ids // RB, 0, block_count - 1)
    block_hit = (block_of[:, None] == jnp.arange(block_count, dtype=jnp.int32)[None, :]).astype(
        jnp.float32
    )
    base_cond = jnp.sum(per_block[:, None, :] * block_hit[None, :, :], axis=2)
    mask_rows = jnp.sum(mask_blocks[:, None, :] * block_hit[None, :, :], axis=2)
    inside = row_inside[None, :, None] * col_inside[None, None, :]
    decay_rate = coarse_decay[0]
    states = initial_states[0]
    jump_field = jnp.zeros_like(states)
    for round_index in range(ITERS):
        current = states
        previous = states
        for substep in range(FSTEPS):
            if substep == 0:
                coef_now, coef_old, weight_scale = (1.0, 0.0, 1.0)
            else:
                coef_now, coef_old, weight_scale = (4.0 / 3.0, -1.0 / 3.0, 2.0 / 3.0)
            iterate = current
            for sweep_index in range(SWEEPS):
                padded = padded_2(iterate, (("sx", 1), ("sy", 2)), 1)
                if sweep_index == 0:
                    conductance = (
                        base_cond[:, :, None] * (1.0 - cond_slope * jnp.tanh(padded)) * inside
                    )
                    weights, denominator = face_weights(conductance, weight_scale)
                    heat_source = (
                        source_gain
                        * mask_rows[substep][1:-1][None, :, None]
                        * power_map
                        * (1.0 + joule_slope * jnp.tanh(current))
                    )
                    right_side = (
                        coef_now * current + coef_old * previous + weight_scale * heat_source
                    )
                iterate = relax(padded, weights, right_side, denominator)
            previous = current
            current = iterate
        if round_index == ITERS - 1:
            following = passed_along(states, "tm", -1)
            jump_field = current - following
        offset = current - decay_rate * states
        unit_map = jnp.ones_like(decay_rate)
        zero_map = jnp.zeros_like(decay_rate)
        scale_pre, shift_pre = entering(
            (decay_rate, offset), "tm", compose_forward, (unit_map, zero_map)
        )
        scale_incl = scale_pre * decay_rate
        shift_incl = decay_rate * shift_pre + offset
        scale_total = broadcast(scale_incl, "tm", lax.axis_size("tm") - 1)
        shift_total = broadcast(shift_incl, "tm", lax.axis_size("tm") - 1)
        first_state = shift_total / (1.0 - scale_total)
        states = scale_pre * first_state + shift_pre
    return (states[None], jump_field[None])


def solution(mesh):
    return jax.shard_map(
        shards,
        mesh=mesh,
        in_specs=(
            P("tm", None, "sx", "sy"),
            P("tm", None, "sx", "sy"),
            P(None, "sx", "sy"),
            P("tm", None, None),
            P(),
            P(),
        ),
        out_specs=(P("tm", None, "sx", "sy"), P("tm", None, "sx", "sy")),
        check_vma=False,
    )
```

profile of v0, /device:TPU:16, one launch (start us, length us, event | category | flops | bytes accessed | tf_op | source)
XLA Modules:
  0.0 2389.5 jit_solution(18325061548936301741)
XLA Ops:
  17.0 6.1 collective-permute-start.3
  39.8 6.3 collective-permute-start.7
  46.1 7.7 collective-permute-done.6
  60.6 6.6 collective-permute-start.11
  67.2 7.3 collective-permute-done.10
  82.0 6.5 collective-permute-start.15
  88.5 7.3 collective-permute-done.14
  103.3 6.3 collective-permute-start.19
  109.6 8.0 collective-permute-done.18
  124.4 6.1 collective-permute-start.23
  130.5 7.4 collective-permute-done.22
  145.1 6.5 collective-permute-start.27
  151.6 7.8 collective-permute-done.26
  167.0 6.1 collective-permute-start.31
  173.1 7.0 collective-permute-done.30
  187.4 6.1 collective-permute-start.35
  193.5 7.8 collective-permute-done.34
  207.9 6.3 collective-permute-start.39
  214.3 8.1 collective-permute-done.38
  229.1 6.1 collective-permute-start.43
  235.2 7.2 collective-permute-done.42
  249.5 6.4 collective-permute-start.47
  256.0 7.6 collective-permute-done.46
  265.6 62.2 %all-gather.6.cloned.1.call-done = f32[64,8,32,128]{3,2,1,0:T(8,128)} async-done(((f32[1,8,32,128]{3,2,1,0:T(8,128)}), f32[64,8,32,128]{3,2,1,0:T(8,128)}) %all-gather.6.cloned.1.call-update) | async-done | bytes 8388624 | tf_op jit(solution)/shard_map/all_gather | solution.py:36
  327.9 313.3 %all-gather.8.cloned.1.call-done = f32[512,32,128]{2,1,0:T(8,128)} async-done(((f32[8,32,128]{2,1,0:T(8,128)}), f32[512,32,128]{2,1,0:T(8,128)}) %all-gather.8.cloned.1.call-update) | async-done | bytes 8388624 | tf_op jit(solution)/shard_map/all_gather | solution.py:36
  641.2 70.5 %while.32 = (s32[]{:T(128)}, f32[8,32,128]{2,1,0:T(8,128)S(1)}, f32[8,32,128]{2,1,0:T(8,128)S(1)}, s32[]{:T(128)}, f32[64,8,32,128]{3,2,1,0:T(8,128)}, /*index=5*/f32[64,8,32,128]{3,2,1,0:T(8,128)}, s32[]{:T(128)}, s32[]{:T(128)}) while((s32[]{:T(128)}, f32[8,32,128]{2,1,0:T(8,128)S(1)}, f32[8,32,128]{2,1,0:T(8,128)S(1)}, ...), condition=%wide.region_4.5_spmd.clone, body=%wide.region_3.4_spmd.clone.sunk | while | flops 229380 | bytes 786541 | solution.py:46
  713.5 545.3 %all-reduce.71.cloned.1.call-done = (f32[8,32,128]{2,1,0:T(8,128)}, f32[8,32,128]{2,1,0:T(8,128)}) async-done(((f32[8,32,128]{2,1,0:T(8,128)}, f32[8,32,128]{2,1,0:T(8,128)}), (f32[8,32,128]{2,1,0:T(8,128)}, f32[8,32,128]{2,1,0:T(8,128)})) %all-reduce.71.cloned.1.call-update) | async-done | bytes 262160 | tf_op jit(solution)/shard_map/psum | solution.py:51
  1393.9 6.1 collective-permute-start.83
  1442.6 6.1 collective-permute-start.95
  1454.7 309.4 %all-gather.10.cloned.1.call-done = f32[512,32,128]{2,1,0:T(8,128)} async-done(((f32[8,32,128]{2,1,0:T(8,128)}), f32[512,32,128]{2,1,0:T(8,128)}) %all-gather.10.cloned.1.call-update) | async-done | bytes 8388624 | tf_op jit(solution)/shard_map/all_gather | solution.py:36
  1764.0 70.0 %while.33 = (s32[]{:T(128)}, f32[8,32,128]{2,1,0:T(8,128)S(1)}, f32[8,32,128]{2,1,0:T(8,128)S(1)}, s32[]{:T(128)}, f32[64,8,32,128]{3,2,1,0:T(8,128)}, /*index=5*/f32[64,8,32,128]{3,2,1,0:T(8,128)}, s32[]{:T(128)}, s32[]{:T(128)}) while((s32[]{:T(128)}, f32[8,32,128]{2,1,0:T(8,128)S(1)}, f32[8,32,128]{2,1,0:T(8,128)S(1)}, ...), condition=%wide.region_8.9_spmd.clone, body=%wide.region_7.8_spmd.clone.sunk | while | flops 229380 | bytes 786541 | solution.py:46
  1835.8 545.5 %all-reduce.69.cloned.1.call-done = (f32[8,32,128]{2,1,0:T(8,128)}, f32[8,32,128]{2,1,0:T(8,128)}) async-done(((f32[8,32,128]{2,1,0:T(8,128)}, f32[8,32,128]{2,1,0:T(8,128)}), (f32[8,32,128]{2,1,0:T(8,128)}, f32[8,32,128]{2,1,0:T(8,128)})) %all-reduce.69.cloned.1.call-update) | async-done | bytes 262160 | tf_op jit(solution)/shard_map/psum | solution.py:51
  (469 shorter events, 424.5 us)
Async XLA Ops:
  7.2 320.7 %all-gather.6.cloned.1.call-start = ((), (), s32[]{:S(2)}) async-start(), calls=%async_computation | async-start | bytes 8519680 | tf_op jit(solution)/shard_map/all_gather | solution.py:36
  7.9 633.3 %all-gather.8.cloned.1.call-start = ((), (), s32[]{:S(2)}) async-start(), calls=%async_computation.1 | async-start | bytes 8519680 | tf_op jit(solution)/shard_map/all_gather | solution.py:36
  15.7 13.0 collective-permute-start.2
  17.0 13.6 collective-permute-start.3
  38.5 15.3 collective-permute-start.6
  39.8 14.7 collective-permute-start.7
  59.3 15.2 collective-permute-start.10
  60.6 15.2 collective-permute-start.11
  80.7 15.1 collective-permute-start.14
  82.0 14.4 collective-permute-start.15
  102.0 15.6 collective-permute-start.18
  103.3 14.7 collective-permute-start.19
  123.1 14.8 collective-permute-start.22
  124.4 14.4 collective-permute-start.23
  143.8 15.6 collective-permute-start.26
  145.1 14.3 collective-permute-start.27
  165.7 14.4 collective-permute-start.30
  167.0 14.3 collective-permute-start.31
  186.1 15.2 collective-permute-start.34
  187.4 14.3 collective-permute-start.35
  206.6 15.8 collective-permute-start.38
  207.9 14.5 collective-permute-start.39
  227.8 14.6 collective-permute-start.42
  229.1 14.3 collective-permute-start.43
  248.2 15.4 collective-permute-start.46
  249.5 15.0 collective-permute-start.47
  265.6 993.2 %all-reduce.71.cloned.1.call-start = ((), (), s32[]{:S(2)}) async-start(), calls=%async_computation.4 | async-start | bytes 524288 | tf_op jit(solution)/shard_map/psum | solution.py:51
  713.4 1050.6 %all-gather.10.cloned.1.call-start = ((), (), s32[]{:S(2)}) async-start(), calls=%async_computation.2 | async-start | bytes 8519680 | tf_op jit(solution)/shard_map/all_gather | solution.py:36
  1438.7 14.2 collective-permute-start.96
  1441.3 10.3 collective-permute-start.94
  1442.6 10.2 collective-permute-start.95
  1454.6 926.7 %all-reduce.69.cloned.1.call-start = ((), (), s32[]{:S(2)}) async-start(), calls=%async_computation.3 | async-start | bytes 524288 | tf_op jit(solution)/shard_map/psum | solution.py:51
  (73 other events, 642.8 us)
Sparse Core Ops, SparseCore 0:
  9.8 318.0 all-gather.5
  330.2 310.9 all-gather.7
  713.5 545.1 all-reduce.70
  1454.7 309.2 all-gather.9
  1835.9 545.3 all-reduce.68
where the time goes:
time: 2390 us
  waiting for transfers between devices  1960 us (82%)
  starting transfers between devices  246 us (10%)
  other arithmetic  163 us (7%)
    psum x2, waiting for transfers between devices, broadcast(): return lax.psum(jnp.where(mine, x, jnp.zeros_like(x)), axis)  1090 us
    all_gather x3, waiting for transfers between devices, entering(): everything = jax.tree.map(lambda part: lax.all_gather(part, axis), x)  685 us
    ppermute x48, starting transfers between devices, padded_2(): after = lax.ppermute(initial, axis, down)  179 us
    select_n x128, other arithmetic, step(): return jax.tree.map(lambda a, b: jnp.where(reached, a, b), new, before)  138 us
    ppermute x48, waiting for transfers between devices, padded_2(): before = lax.ppermute(last, axis, up)  118 us
    ppermute x48, starting transfers between devices, padded_2(): before = lax.ppermute(last, axis, up)  64.5 us
    ppermute x48, waiting for transfers between devices, padded_2(): after = lax.ppermute(initial, axis, down)  62 us
  transfers between devices with their start and end apart: 102, of which 73 were waited for; matrix products, arithmetic and copies ran while one was open for 1% of the time, Pallas kernels for 0%

commit v1 on v0

v1 whole, which is shorter than its diff:
```python
import functools

import jax
import jax.numpy as jnp
from jax import lax
from jax.experimental import pallas as pl
from jax.experimental.pallas import tpu as pltpu
from jax.sharding import PartitionSpec as P

RB = 8
REGIONS = 4
FSTEPS = 4
SWEEPS = 3
ITERS = 2
cond_slope = 0.25
joule_slope = 0.3

HALO = FSTEPS * SWEEPS
ROWS = 32
LAYERS = 8
COLS = 128
BOX = ROWS + HALO
GROUPS = 3
PACK = 15
WIDE = 40
VMEM = pltpu.VMEM


def spec():
    return pl.BlockSpec(memory_space=VMEM)


def sspec():
    return pl.BlockSpec(memory_space=pltpu.SMEM)


def plane(*shape):
    return jax.ShapeDtypeStruct((*shape, LAYERS, COLS), jnp.float32)


def lanes():
    return lax.broadcasted_iota(jnp.int32, (LAYERS, COLS), 1)


def layers():
    return lax.broadcasted_iota(jnp.int32, (LAYERS, COLS), 0)


def box_row(r, own, halo):
    r = min(r, BOX - 1)
    return own[r] if r < ROWS else halo[BOX - 1 - r]


def packed_row(i, row, shift):
    lane = lanes()
    parts = [pltpu.roll(row(g * PACK + i), shift + g * WIDE, 1) for g in range(GROUPS)]
    return jnp.where(lane < WIDE, parts[0], jnp.where(lane < 2 * WIDE, parts[1], parts[2]))


def own_shift(sy):
    return jnp.where(sy == 0, 24, 12)


def sent_shift(sy):
    return jnp.where(sy == 0, 12, 24)


def advance(n, packed, state, tmp, wx, wyp, wzp, inv, rhs, base, heat, power):
    lane = lanes()
    layer = layers()
    edge = jnp.where(layer == 0, 1.0, 0.0)
    if not packed:
        edge = edge + jnp.where(lane == 0, 1.0, 0.0) + jnp.where(lane == COLS - 1, 1.0, 0.0)

    def step(m, carry):
        first = m == 0
        now = lax.rem(m, 2)
        old = 1 - now
        coef_now = jnp.where(first, 1.0, 4.0 / 3.0).astype(jnp.float32)
        coef_old = jnp.where(first, 0.0, -1.0 / 3.0).astype(jnp.float32)
        half = jnp.where(first, 0.5, 1.0 / 3.0).astype(jnp.float32)
        cond = []
        for r in range(n):
            cur = state[now, r]
            tanh = jnp.tanh(cur)
            cond.append((half * base(r)) * (1.0 - cond_slope * tanh))
            source = (half * heat(m, r)) * power[r] * (1.0 + joule_slope * tanh)
            rhs[r] = coef_now * cur + coef_old * state[old, r] + source
        faces = []
        for r in range(n):
            if r:
                faces.append(cond[r - 1] + cond[r])
            elif packed:
                faces.append(jnp.where(lane < WIDE, 0.0, cond[0] + pltpu.roll(cond[n - 1], WIDE, 1)))
            else:
                faces.append(None)
        faces.append(cond[n - 1] + pltpu.roll(cond[0], COLS - WIDE, 1) if packed else None)
        for r in range(n + 1):
            if faces[r] is not None:
                wx[r] = faces[r]
        for r in range(n):
            c = cond[r]
            north = c + pltpu.roll(c, COLS - 1, 1)
            if not packed:
                north = jnp.where(lane == COLS - 1, 0.0, north)
            up = jnp.where(layer == LAYERS - 1, 0.0, 0.5 * (c + pltpu.roll(c, LAYERS - 1, 0)))
            total = north + pltpu.roll(north, 1, 1) + up + pltpu.roll(up, 1, 0) + edge * c
            low = faces[r]
            if r == 0:
                low = c if low is None else low + jnp.where(lane < WIDE, c, 0.0)
            high = c if faces[r + 1] is None else faces[r + 1]
            wyp[r] = north
            wzp[r] = up
            inv[r] = 1.0 / (1.0 + (total + low + high))

        def sweep(source, store):
            vs = [source(r) for r in range(n)]
            for r in range(n):
                v = vs[r]
                north = wyp[r]
                up = wzp[r]
                acc = rhs[r] + pltpu.roll(north * v, 1, 1) + north * pltpu.roll(v, COLS - 1, 1)
                acc = acc + pltpu.roll(up * v, 1, 0) + up * pltpu.roll(v, LAYERS - 1, 0)
                if r:
                    acc = acc + wx[r] * vs[r - 1]
                elif packed:
                    acc = acc + wx[0] * pltpu.roll(vs[n - 1], WIDE, 1)
                if r < n - 1:
                    acc = acc + wx[r + 1] * vs[r + 1]
                elif packed:
                    acc = acc + wx[n] * pltpu.roll(vs[0], COLS - WIDE, 1)
                store(r, acc * inv[r])

        def into(ref, *at):
            def put(r, value):
                ref[(*at, r)] = value
            return put

        sweep(lambda r: state[now, r], into(tmp, 0))
        sweep(lambda r: tmp[0, r], into(tmp, 1))
        sweep(lambda r: tmp[1, r], into(state, old))
        return carry

    lax.fori_loop(0, FSTEPS, step, 0)


def scratch(n):
    return [VMEM((2, n, LAYERS, COLS), jnp.float32), VMEM((2, n, LAYERS, COLS), jnp.float32)] + [
        VMEM((n + 1, LAYERS, COLS), jnp.float32) for _ in range(5)
    ]


def native_row(here, r):
    return jnp.where(here[0] == 0, r, ROWS - 1 - r)


def turn_kernel(count, here, *refs):
    ins, outs, send = refs[:count], refs[count:2 * count], refs[2 * count]
    for k in range(count):
        for r in range(ROWS):
            row = ins[k][pl.ds(native_row(here, r), LAYERS, stride=ROWS), :]
            outs[k][r] = row
            if r >= ROWS - HALO:
                send[k, r - (ROWS - HALO)] = row


def turn(here, arrays):
    count = len(arrays)
    return pl.pallas_call(
        functools.partial(turn_kernel, count),
        out_shape=[plane(ROWS)] * count + [plane(count, HALO)],
        in_specs=[sspec()] + [spec()] * count,
        out_specs=[spec()] * (count + 1),
        name="turn",
    )(here, *[a.reshape(LAYERS * ROWS, COLS) for a in arrays])


def pack_kernel(count, here, *refs):
    owns, halo, out = refs[:count], refs[count], refs[count + 1]
    shift = sent_shift(here[1])
    for k in range(count):
        for i in range(PACK):
            out[k, i] = packed_row(i, lambda r: box_row(r, owns[k], halo.at[k]), shift)


def pack(here, owns, halo):
    count = len(owns)
    return pl.pallas_call(
        functools.partial(pack_kernel, count),
        out_shape=plane(count, PACK),
        in_specs=[sspec()] + [spec()] * (count + 1),
        out_specs=spec(),
        name="pack",
    )(here, *owns, halo)


def main_kernel(first, here, mask, base, own, halo, *refs):
    if first:
        power_own, decay, end, band, power_box, power_band, decay_box, *work = refs
        for r in range(BOX):
            power_box[r] = box_row(r, power_own, halo.at[1])
        for r in range(ROWS):
            decay_box[r] = decay[pl.ds(native_row(here, r), LAYERS, stride=ROWS), :]
    else:
        power_box, end, band, *work = refs
    state = work[0]
    shift = own_shift(here[1])
    for r in range(BOX):
        row = box_row(r, own, halo.at[0])
        state[0, r] = row
        state[1, r] = row
    for i in range(PACK):
        band[i] = packed_row(i, lambda r: box_row(r, own, halo.at[0]), shift)
        if first:
            power_band[i] = packed_row(i, lambda r: box_row(r, power_own, halo.at[1]), shift)
    advance(
        BOX, False, *work,
        lambda r: base[r // RB],
        lambda m, r: mask[m, r // RB],
        power_box,
    )
    for r in range(ROWS):
        end[r] = state[0, r]


def main(here, mask, base, own, halo, first, extra):
    outs = [plane(ROWS), plane(PACK)]
    if first:
        outs = outs + [plane(BOX), plane(PACK), plane(ROWS)]
    return pl.pallas_call(
        functools.partial(main_kernel, first),
        out_shape=outs,
        in_specs=[sspec(), sspec()] + [spec()] * (3 + len(extra)),
        out_specs=[spec()] * len(outs),
        scratch_shapes=scratch(BOX),
        cost_estimate=pl.CostEstimate(flops=20_000_000, bytes_accessed=4_000_000, transcendentals=400_000),
        name="propagate_rows",
    )(here, mask, base, own, halo, *extra)


def band_kernel(first, here, mask, base, end, band, other, own, decay, *refs):
    if first:
        power_own, power, offset_box, send, *work = refs
    else:
        power, offset_before, send, jump, *work = refs
    state = work[0]
    lane = lanes()
    slot = lane - jnp.where(lane < WIDE, 0, jnp.where(lane < 2 * WIDE, WIDE, 2 * WIDE))
    left = here[1] == 0
    here_low = jnp.where(left, 0, 12)
    here_high = jnp.where(left, 24, 36)
    mine = (slot >= here_low) & (slot < here_high)
    for i in range(PACK):
        row = jnp.where(mine, band[i], other[0, i])
        state[0, i] = row
        state[1, i] = row
        if first:
            power[i] = jnp.where(mine, power_own[i], other[1, i])

    def by_group(value):
        return jnp.where(lane < WIDE, value(0), jnp.where(lane < 2 * WIDE, value(1), value(2)))

    def block(g, i):
        return min(g * PACK + i, BOX - 1) // RB

    advance(
        PACK, True, *work,
        lambda i: by_group(lambda g: base[block(g, i)]),
        lambda m, i: by_group(lambda g: mask[m, block(g, i)]),
        power,
    )
    back = COLS - own_shift(here[1])
    border = ((lane >= COLS - HALO) & left) | ((lane < HALO) & jnp.logical_not(left))
    for r in range(ROWS):
        moved = pltpu.roll(state[0, r % PACK], lax.rem(back + (2 * COLS - (r // PACK) * WIDE), COLS), 1)
        f = jnp.where(border, moved, end[r])
        u = own[r]
        d = decay[r]
        x = native_row(here, r)
        if first:
            offset = f - d * u
            offset_box[r] = offset
            at = lax.div(x, 4) * 8 + lax.rem(x, 4)
            send[pl.ds(at, LAYERS, stride=64), :] = d
            send[pl.ds(at + 4, LAYERS, stride=64), :] = offset
        else:
            du = d * u
            send[pl.ds(x, LAYERS, stride=ROWS), :] = f - du
            jump[pl.ds(x, LAYERS, stride=ROWS), :] = f - (du + offset_before[r])


def border(here, mask, base, end, band, other, own, decay, first, extra):
    if first:
        outs = [plane(PACK), plane(ROWS), jax.ShapeDtypeStruct((512, COLS), jnp.float32)]
    else:
        outs = [jax.ShapeDtypeStruct((256, COLS), jnp.float32)] * 2
    return pl.pallas_call(
        functools.partial(band_kernel, first),
        out_shape=outs,
        in_specs=[sspec(), sspec()] + [spec()] * (6 + len(extra)),
        out_specs=[spec()] * len(outs),
        scratch_shapes=scratch(PACK),
        name="propagate_band",
    )(here, mask, base, end, band, other, own, decay, *extra)


def cycle_kernel(slabs, rate, offset, out):
    scale = rate(0)
    shift = offset(0)
    for k in range(1, slabs):
        d = rate(k)
        scale = scale * d
        shift = d * shift + offset(k)
    u = shift / (1.0 - scale)
    out[0] = u
    for k in range(slabs - 1):
        u = rate(k) * u + offset(k)
        out[k + 1] = u


def cycle_first(slabs, both, out):
    cycle_kernel(slabs, lambda k: both[k, 0:4], lambda k: both[k, 4:8], out)


def cycle_later(slabs, both, offset, out):
    cycle_kernel(slabs, lambda k: both[k, 0:4], lambda k: offset[k], out)


def cycle(both, offset):
    slabs = both.shape[0]
    args = (both,) if offset is None else (both, offset)
    return pl.pallas_call(
        functools.partial(cycle_first if offset is None else cycle_later, slabs),
        out_shape=jax.ShapeDtypeStruct((slabs, 4, COLS), jnp.float32),
        in_specs=[spec()] * len(args),
        out_specs=spec(),
        name="cycle",
    )(*args)


def base_rows(region_ids, region_conductivity):
    labels = jnp.arange(REGIONS, dtype=jnp.int32)
    chosen = (region_ids[:, :, None] == labels[None, None, :]).astype(jnp.float32)
    return jnp.sum(chosen * region_conductivity[None, None, :], axis=2)


SWAP = [(0, 1), (1, 0)]


def shards(initial_states, coarse_decay, power_map, power_mask, region_ids, region_conductivity):
    slabs = lax.axis_size("tm")
    sx = lax.axis_index("sx")
    here = jnp.stack([sx, lax.axis_index("sy")]).astype(jnp.int32)
    per_block = base_rows(region_ids, region_conductivity).T
    per_block = jnp.where(sx == 0, per_block, per_block[::-1])
    base = jnp.broadcast_to(per_block[:, :, None], (*per_block.shape, COLS))
    mask = power_mask[0].astype(jnp.float32)
    mask = jnp.where(sx == 0, mask, mask[:, ::-1])
    decay_native = coarse_decay.reshape(LAYERS * ROWS, COLS)

    own, power_own, send = turn(here, [initial_states, power_map])
    halo = lax.ppermute(send, "sx", SWAP)
    sent = pack(here, [own, power_own], halo)
    other = lax.ppermute(sent, "sy", SWAP)
    end, band, power_box, power_band_own, decay = main(
        here, mask, base, own, halo, True, (power_own, decay_native)
    )
    power_band, offset, both = border(
        here, mask, base, end, band, other, own, decay, True, (power_band_own,)
    )
    both = lax.all_to_all(both.reshape(slabs, 8, COLS), "tm", 0, 0, tiled=True)
    states = lax.all_to_all(cycle(both, None), "tm", 0, 0, tiled=True)

    own, send = turn(here, [states])
    halo = lax.ppermute(send, "sx", SWAP)
    sent = pack(here, [own], halo)
    other = lax.ppermute(sent, "sy", SWAP)
    end, band = main(here, mask, base, own, halo, False, (power_box,))
    later, jump = border(
        here, mask, base, end, band, other, own, decay, False, (power_band, offset)
    )
    later = lax.all_to_all(later.reshape(slabs, 4, COLS), "tm", 0, 0, tiled=True)
    states = lax.all_to_all(cycle(both, later), "tm", 0, 0, tiled=True)
    shape = (1, LAYERS, ROWS, COLS)
    return states.reshape(shape), jump.reshape(shape)


def solution(mesh):
    return jax.shard_map(
        shards,
        mesh=mesh,
        in_specs=(
            P("tm", None, "sx", "sy"),
            P("tm", None, "sx", "sy"),
            P(None, "sx", "sy"),
            P("tm", None, None),
            P(),
            P(),
        ),
        out_specs=(P("tm", None, "sx", "sy"), P("tm", None, "sx", "sy")),
        check_vma=False,
    )
```

time: 2390 us -> 113 us (0.05)
  waiting for transfers between devices: 1960 us -> 1.79 us
  starting transfers between devices: 246 us -> 3.74 us
  other arithmetic: 163 us -> 1.3 us
  blocking collectives: 0 us -> 72.1 us
  Pallas kernels: 0 us -> 26.7 us
    psum x2 -> x0, waiting for transfers between devices: 1090 us -> none  [broadcast(): return lax.psum(jnp.where(mine, x, jnp.zeros_like(x)), axis)]
    all_gather x3 -> x0, waiting for transfers between devices: 685 us -> none  [entering(): everything = jax.tree.map(lambda part: lax.all_gather(part, axis), x)]
    ppermute x97 -> x4, starting transfers between devices: 246 us -> 3.74 us  [the longest x2 3.74 us: shards(): other = lax.ppermute(sent, 'sy', SWAP)]
    ppermute x97 -> x4, waiting for transfers between devices: 180 us -> 1.79 us  [the longest x2 1.44 us: shards(): halo = lax.ppermute(send, 'sx', SWAP)]
    select_n x130 -> x2, other arithmetic: 141 us -> 0.6 us  [the longest x1 0.6 us: shards(): mask = jnp.where(sx == 0, mask, mask[:, ::-1])]
    all_to_all x0 -> x4, blocking collectives: none -> 72.1 us  [the longest x1 24.2 us: shards(): both = lax.all_to_all(both.reshape(slabs, 8, COLS), 'tm', 0, 0, tiled=True)]
    pallas_call x0 -> x10, Pallas kernels: none -> 26.7 us  [the longest x2 8.02 us: main(): pl.pallas_call(functools.partial(main_kernel, first), out_shape=outs, in_...]
  transfers between devices with their start and end apart: 102 -> 4, of which waited for: 73 -> 2; matrix products, arithmetic and copies ran while one was open for 1% -> 1% of each run, Pallas kernels for 0% -> 7%
where the time goes in v1:
time: 113 us; the launch traced here: 112 us
  blocking collectives  72.1 us (64%)
  Pallas kernels  26.7 us (24%)
  local copies, waits for them, and re-layouts  5.42 us (5%)
  starting transfers between devices  3.74 us (3%)
  waiting for transfers between devices  1.79 us (2%)
  other arithmetic  1.3 us (1%)
    all_to_all x1, blocking collectives, shards(): both = lax.all_to_all(both.reshape(slabs, 8, COLS), 'tm', 0, 0, tiled=True)  24.2 us
    all_to_all x1, blocking collectives, shards(): states = lax.all_to_all(cycle(both, None), 'tm', 0, 0, tiled=True)  16.5 us
    all_to_all x1, blocking collectives, shards(): lax.all_to_all(later.reshape(slabs, 4, COLS), 'tm', 0, 0, tiled=True)  16 us
    all_to_all x1, blocking collectives, shards(): states = lax.all_to_all(cycle(both, later), 'tm', 0, 0, tiled=True)  15.4 us
    pallas_call x2, Pallas kernels, main(): pl.pallas_call(functools.partial(main_kernel, first), out_shape=outs, in_...  8.02 us
    pallas_call x2, Pallas kernels, border(): pl.pallas_call(functools.partial(band_kernel, first), out_shape=outs, in_...  7.69 us
    unnamed x15, local copies, waits for them, and re-layouts  4.51 us
    pallas_call x2, Pallas kernels, cycle(): pl.pallas_call(functools.partial(cycle_first if offset is None else cycle...  3.78 us
  transfers between devices with their start and end apart: 4, of which 2 were waited for; matrix products, arithmetic and copies ran while one was open for 1% of the time, Pallas kernels for 7%

profile of v1, /device:TPU:16, one launch (start us, length us, event | category | flops | bytes accessed | tf_op | source)
XLA Modules:
  0.0 111.7 jit_solution(18163658918734197004)
XLA Ops:
  0.6 0.6 pad_add_fusion.here
  1.3 2.0 %turn.2 = (f32[32,8,128]{2,1,0:T(8,128)}, f32[32,8,128]{2,1,0:T(8,128)}, f32[2,12,8,128]{3,2,1,0:T(8,128)}) custom-call(s32[2]{0:T(128)} %pad_add_fusion.here, f32[256,128]{1,0:T(8,128)} %bitcast.19, f32[256,128]{1,0:T(8,128)} %bitcast.20), custom_call_target="tpu_custom_call" | custom-call | tf_op jit(solution)/shard_map/turn/pallas_call | solution.py:169
  3.3 0.6 copy-done.6
  3.9 0.1 select_reduce_fusion
  4.0 0.1 rev.7
  4.1 0.7 copy-done.4
  4.7 0.1 rev.6
  4.8 0.1 copy.8
  4.9 0.6 copy-done.1
  5.5 1.8 %pack.2 = f32[2,15,8,128]{3,2,1,0:T(8,128)} custom-call(s32[2]{0:T(128)} %pad_add_fusion.here, f32[32,8,128]{2,1,0:T(8,128)} %get-tuple-element.19.own.refs_0_, f32[32,8,128]{2,1,0:T(8,128)} %get-tuple-element.21.refs_0_.refs_1_, f32[2,12,8,128]{3,2,1,0:T(8,128)} %copy-done.1), custom_call_target="tpu_custom_call" | custom-call | tf_op jit(solution)/shard_map/pack/pallas_call | solution.py:188
  7.4 2.1 %collective-permute-start.1 = (f32[2,15,8,128]{3,2,1,0:T(8,128)}, f32[2,15,8,128]{3,2,1,0:T(8,128)S(1)}, u32[]{:S(2)}, u32[]{:S(2)}) collective-permute-start(f32[2,15,8,128]{3,2,1,0:T(8,128)} %pack.2), channel_id=1, source_target_pairs={{0,1},{1,0},{2,3},{3,2},{4,5},{5,4},{6,7},{7,6},{8,9},{9,8},{10,11... | collective-permute-start | bytes 368648 | tf_op jit(solution)/shard_map/ppermute | solution.py:364
  9.4 0.6 broadcast_select_fusion.1.mask
  10.0 0.7 broadcast_in_dim.2.base
  10.7 4.1 %propagate_rows.2 = (f32[32,8,128]{2,1,0:T(8,128)}, f32[15,8,128]{2,1,0:T(8,128)}, f32[44,8,128]{2,1,0:T(8,128)}, f32[15,8,128]{2,1,0:T(8,128)}, f32[32,8,128]{2,1,0:T(8,128)}) custom-call(s32[2]{0:T(128)} %pad_add_fusion.here, f32[4,8]{1,0:T(4,128)} %broadcast_select_fusion.1.mask, f32[8,8,128]{2,1,0:T(8,128)} %broadcast_in_dim.2.base, ...), custom_call_target="tpu_custom_call" | custom-call | flops 20000000 | bytes 4000000 | tf_op jit(solution)/shard_map/propagate_rows/pallas_call | solution.py:230
  14.8 0.6 copy-done
  15.5 3.8 %propagate_band.2 = (f32[15,8,128]{2,1,0:T(8,128)}, f32[32,8,128]{2,1,0:T(8,128)}, f32[512,128]{1,0:T(8,128)}) custom-call(s32[2]{0:T(128)} %pad_add_fusion.here, f32[4,8]{1,0:T(4,128)} %broadcast_select_fusion.1.mask, f32[8,8,128]{2,1,0:T(8,128)} %broadcast_in_dim.2.base, f32[32,8,128]{2,1,0:T(8,128)} %get-tuple-element.22.end, ...), custom_call_target="tpu_custom_call" | custom-call | tf_op jit(solution)/shard_map/propagate_band/pallas_call | solution.py:297
  19.3 24.2 %all_to_all.20.both = f32[64,8,128]{2,1,0:T(8,128)} all-to-all(f32[64,8,128]{2,1,0:T(8,128)} %bitcast.18), channel_id=1, replica_groups=mesh['tm'=64,'sx'=2,'sy'=2] {'tm'}, dimensions={0} | all-to-all | bytes 524288 | tf_op jit(solution)/shard_map/all_to_all | solution.py:371
  43.5 1.9 %cycle.2 = f32[64,4,128]{2,1,0:T(4,128)} custom-call(f32[64,8,128]{2,1,0:T(8,128)} %all_to_all.20.both), custom_call_target="tpu_custom_call" | custom-call | tf_op jit(solution)/shard_map/cycle/pallas_call | solution.py:332
  45.4 16.5 %all_to_all.21 = f32[64,4,128]{2,1,0:T(4,128)} all-to-all(f32[64,4,128]{2,1,0:T(4,128)} %cycle.2), channel_id=1, replica_groups=mesh['tm'=64,'sx'=2,'sy'=2] {'tm'}, dimensions={0} | all-to-all | bytes 262144 | tf_op jit(solution)/shard_map/all_to_all | solution.py:372
  61.9 1.7 %turn.3 = (f32[32,8,128]{2,1,0:T(8,128)}, f32[1,12,8,128]{3,2,1,0:T(8,128)}) custom-call(s32[2]{0:T(128)} %pad_add_fusion.here, f32[256,128]{1,0:T(8,128)} %bitcast.16), custom_call_target="tpu_custom_call" | custom-call | tf_op jit(solution)/shard_map/turn/pallas_call | solution.py:169
  63.6 1.4 %collective-permute-done.2.halo.refs_1_ = f32[1,12,8,128]{3,2,1,0:T(8,128)S(1)} collective-permute-done((f32[1,12,8,128]{3,2,1,0:T(8,128)}, f32[1,12,8,128]{3,2,1,0:T(8,128)S(1)}, u32[]{:S(2)}, u32[]{:S(2)}) %collective-permute-start.2) | collective-permute-done | bytes 49184 | tf_op jit(solution)/shard_map/ppermute | solution.py:375
  65.0 0.6 copy-done.3
  65.7 1.7 %pack.3 = f32[1,15,8,128]{3,2,1,0:T(8,128)} custom-call(s32[2]{0:T(128)} %pad_add_fusion.here, f32[32,8,128]{2,1,0:T(8,128)} %get-tuple-element.27.own.refs_0_, f32[1,12,8,128]{3,2,1,0:T(8,128)} %copy-done.3), custom_call_target="tpu_custom_call" | custom-call | tf_op jit(solution)/shard_map/pack/pallas_call | solution.py:188
  67.3 1.7 %collective-permute-start.3 = (f32[1,15,8,128]{3,2,1,0:T(8,128)}, f32[1,15,8,128]{3,2,1,0:T(8,128)S(1)}, u32[]{:S(2)}, u32[]{:S(2)}) collective-permute-start(f32[1,15,8,128]{3,2,1,0:T(8,128)} %pack.3), channel_id=1, source_target_pairs={{0,1},{1,0},{2,3},{3,2},{4,5},{5,4},{6,7},{7,6},{8,9},{9,8},{10,11... | collective-permute-start | bytes 184328 | tf_op jit(solution)/shard_map/ppermute | solution.py:377
  69.0 3.9 %propagate_rows.3 = (f32[32,8,128]{2,1,0:T(8,128)}, f32[15,8,128]{2,1,0:T(8,128)}) custom-call(s32[2]{0:T(128)} %pad_add_fusion.here, f32[4,8]{1,0:T(4,128)} %broadcast_select_fusion.1.mask, f32[8,8,128]{2,1,0:T(8,128)} %broadcast_in_dim.2.base, f32[32,8,128]{2,1,0:T(8,128)} %get-tuple-element.27.own.refs_0_, f32[1,12,8,128]{3,2,1,0:T(8,128)} %copy-done.3, ...), custom_call_target="tpu_custom_call" | custom-call | flops 20000000 | bytes 4000000 | tf_op jit(solution)/shard_map/propagate_rows/pallas_call | solution.py:230
  72.9 0.3 collective-permute-done.3.other
  73.3 0.6 copy-done.2
  73.9 3.8 %propagate_band.3 = (f32[256,128]{1,0:T(8,128)}, f32[256,128]{1,0:T(8,128)}) custom-call(s32[2]{0:T(128)} %pad_add_fusion.here, f32[4,8]{1,0:T(4,128)} %broadcast_select_fusion.1.mask, f32[8,8,128]{2,1,0:T(8,128)} %broadcast_in_dim.2.base, f32[32,8,128]{2,1,0:T(8,128)} %get-tuple-element.30.end, f32[15,8,128]{2,1,0:T(8,128)} %get-tuple-element.31.band, ...), custom_call_target="tpu_custom_call" | custom-call | tf_op jit(solution)/shard_map/propagate_band/pallas_call | solution.py:297
  77.7 16.0 %all_to_all.22.offset = f32[64,4,128]{2,1,0:T(4,128)} all-to-all(f32[64,4,128]{2,1,0:T(4,128)} %bitcast.21), channel_id=1, replica_groups=mesh['tm'=64,'sx'=2,'sy'=2] {'tm'}, dimensions={0} | all-to-all | bytes 262144 | tf_op jit(solution)/shard_map/all_to_all | solution.py:382
  93.8 1.9 %cycle.3 = f32[64,4,128]{2,1,0:T(4,128)} custom-call(f32[64,8,128]{2,1,0:T(8,128)} %all_to_all.20.both, f32[64,4,128]{2,1,0:T(4,128)} %all_to_all.22.offset), custom_call_target="tpu_custom_call" | custom-call | tf_op jit(solution)/shard_map/cycle/pallas_call | solution.py:332
  95.7 15.4 %all_to_all.23 = f32[64,4,128]{2,1,0:T(4,128)S(1)} all-to-all(f32[64,4,128]{2,1,0:T(4,128)} %cycle.3), channel_id=1, replica_groups=mesh['tm'=64,'sx'=2,'sy'=2] {'tm'}, dimensions={0} | all-to-all | bytes 262144 | tf_op jit(solution)/shard_map/all_to_all | solution.py:383
  111.0 0.7 copy.10
  (14 shorter events, 0.0 us)
Async XLA Ops:
  1.3 2.0 %copy-start.5 = (s32[8,8]{1,0:T(8,128)S(1)}, s32[8,8]{1,0:T(8,128)}, u32[]{:S(2)}) copy-start(s32[8,8]{1,0:T(8,128)} %param.10) | copy-start | bytes 772
  3.2 0.7 copy-start.6
  3.2 1.7 %collective-permute-start = (f32[2,12,8,128]{3,2,1,0:T(8,128)}, f32[2,12,8,128]{3,2,1,0:T(8,128)S(1)}, u32[]{:S(2)}, u32[]{:S(2)}) collective-permute-start(f32[2,12,8,128]{3,2,1,0:T(8,128)} %get-tuple-element.20), channel_id=1, source_target_pairs={{0,2},{2,0},{1,3},{3,1},{4,6},{6,4},{5,7},{7,5},{8,10},{10,8},{9,1... | collective-permute-start | bytes 294920 | tf_op jit(solution)/shard_map/ppermute | solution.py:362
  4.0 0.7 copy-start.4
  4.9 0.6 copy-start.1
  7.4 7.4 %collective-permute-start.1 = (f32[2,15,8,128]{3,2,1,0:T(8,128)}, f32[2,15,8,128]{3,2,1,0:T(8,128)S(1)}, u32[]{:S(2)}, u32[]{:S(2)}) collective-permute-start(f32[2,15,8,128]{3,2,1,0:T(8,128)} %pack.2), channel_id=1, source_target_pairs={{0,1},{1,0},{2,3},{3,2},{4,5},{5,4},{6,7},{7,6},{8,9},{9,8},{10,11... | collective-permute-start | bytes 368648 | tf_op jit(solution)/shard_map/ppermute | solution.py:364
  14.8 0.7 copy-start
  63.6 1.4 %collective-permute-start.2 = (f32[1,12,8,128]{3,2,1,0:T(8,128)}, f32[1,12,8,128]{3,2,1,0:T(8,128)S(1)}, u32[]{:S(2)}, u32[]{:S(2)}) collective-permute-start(f32[1,12,8,128]{3,2,1,0:T(8,128)} %get-tuple-element.28), channel_id=1, source_target_pairs={{0,2},{2,0},{1,3},{3,1},{4,6},{6,4},{5,7},{7,5},{8,10},{10,8},{9,1... | collective-permute-start | bytes 147464 | tf_op jit(solution)/shard_map/ppermute | solution.py:375
  65.0 0.6 copy-start.3
  67.3 5.9 %collective-permute-start.3 = (f32[1,15,8,128]{3,2,1,0:T(8,128)}, f32[1,15,8,128]{3,2,1,0:T(8,128)S(1)}, u32[]{:S(2)}, u32[]{:S(2)}) collective-permute-start(f32[1,15,8,128]{3,2,1,0:T(8,128)} %pack.3), channel_id=1, source_target_pairs={{0,1},{1,0},{2,3},{3,2},{4,5},{5,4},{6,7},{7,6},{8,9},{9,8},{10,11... | collective-permute-start | bytes 184328 | tf_op jit(solution)/shard_map/ppermute | solution.py:377
  73.3 0.6 copy-start.2

commit v2 on v1

--- a/solution.py
+++ b/solution.py
@@ -171,6 +171,7 @@
         out_shape=[plane(ROWS)] * count + [plane(count, HALO)],
         in_specs=[sspec()] + [spec()] * count,
         out_specs=[spec()] * (count + 1),
+        compiler_params=pltpu.CompilerParams(vmem_limit_bytes=8 * 1024 * 1024),
         name="turn",
     )(here, *[a.reshape(LAYERS * ROWS, COLS) for a in arrays])
 
@@ -190,6 +191,7 @@
         out_shape=plane(count, PACK),
         in_specs=[sspec()] + [spec()] * (count + 1),
         out_specs=spec(),
+        compiler_params=pltpu.CompilerParams(vmem_limit_bytes=8 * 1024 * 1024),
         name="pack",
     )(here, *owns, halo)
 
@@ -234,6 +236,7 @@
         out_specs=[spec()] * len(outs),
         scratch_shapes=scratch(BOX),
         cost_estimate=pl.CostEstimate(flops=20_000_000, bytes_accessed=4_000_000, transcendentals=400_000),
+        compiler_params=pltpu.CompilerParams(vmem_limit_bytes=8 * 1024 * 1024),
         name="propagate_rows",
     )(here, mask, base, own, halo, *extra)
 
@@ -300,6 +303,7 @@
         in_specs=[sspec(), sspec()] + [spec()] * (6 + len(extra)),
         out_specs=[spec()] * len(outs),
         scratch_shapes=scratch(PACK),
+        compiler_params=pltpu.CompilerParams(vmem_limit_bytes=8 * 1024 * 1024),
         name="propagate_band",
     )(here, mask, base, end, band, other, own, decay, *extra)
 
@@ -334,6 +338,7 @@
         out_shape=jax.ShapeDtypeStruct((slabs, 4, COLS), jnp.float32),
         in_specs=[spec()] * len(args),
         out_specs=spec(),
+        compiler_params=pltpu.CompilerParams(vmem_limit_bytes=8 * 1024 * 1024),
         name="cycle",
     )(*args)
 

time: 113 us -> 98.5 us (0.87)
  Pallas kernels: 26.7 us -> 14.7 us
  waiting for transfers between devices: 1.79 us -> 5.08 us
  blocking collectives: 72.1 us -> 70.4 us
  local copies, waits for them, and re-layouts: 5.42 us -> 3.99 us
  other arithmetic: 1.3 us -> 0.16 us
    ppermute x2, waiting for transfers between devices: 0.35 us -> 3.86 us  [shards(): other = lax.ppermute(sent, 'sy', SWAP)]
    pallas_call x2, Pallas kernels: 3.78 us -> 0.54 us  [cycle(): pl.pallas_call(functools.partial(cycle_first if offset is None else cycle...]
    pallas_call x2, Pallas kernels: 8.02 us -> 5.76 us  [main(): pl.pallas_call(functools.partial(main_kernel, first), out_shape=outs, in_...]
    pallas_call x2, Pallas kernels: 3.71 us -> 1.5 us  [turn(): pl.pallas_call(functools.partial(turn_kernel, count), out_shape=[plane(RO...]
    pallas_call x2, Pallas kernels: 3.49 us -> 1.36 us  [pack(): pl.pallas_call(functools.partial(pack_kernel, count), out_shape=plane(cou...]
    pallas_call x2, Pallas kernels: 7.69 us -> 5.57 us  [border(): pl.pallas_call(functools.partial(band_kernel, first), out_shape=outs, in_...]
    unnamed x15 -> x13, local copies, waits for them, and re-layouts: 4.51 us -> 3.68 us
  transfers between devices with their start and end apart: 4 -> 4, of which waited for: 2 -> 3; matrix products, arithmetic and copies ran while one was open for 1% -> 0% of each run, Pallas kernels for 7% -> 6%
where the time goes in v2:
time: 98.5 us; the launch traced here: 98.2 us
  blocking collectives  70.4 us (71%)
  Pallas kernels  14.7 us (15%)
  waiting for transfers between devices  5.08 us (5%)
  local copies, waits for them, and re-layouts  3.99 us (4%)
  starting transfers between devices  3.06 us (3%)
    all_to_all x1, blocking collectives, shards(): both = lax.all_to_all(both.reshape(slabs, 8, COLS), 'tm', 0, 0, tiled=True)  24.1 us
    all_to_all x1, blocking collectives, shards(): states = lax.all_to_all(cycle(both, None), 'tm', 0, 0, tiled=True)  16.2 us
    all_to_all x1, blocking collectives, shards(): lax.all_to_all(later.reshape(slabs, 4, COLS), 'tm', 0, 0, tiled=True)  15.1 us
    all_to_all x1, blocking collectives, shards(): states = lax.all_to_all(cycle(both, later), 'tm', 0, 0, tiled=True)  15.1 us
    pallas_call x2, Pallas kernels, main(): pl.pallas_call(functools.partial(main_kernel, first), out_shape=outs, in_...  5.76 us
    pallas_call x2, Pallas kernels, border(): pl.pallas_call(functools.partial(band_kernel, first), out_shape=outs, in_...  5.57 us
    ppermute x2, waiting for transfers between devices, shards(): other = lax.ppermute(sent, 'sy', SWAP)  3.86 us
    unnamed x13, local copies, waits for them, and re-layouts  3.68 us
  transfers between devices with their start and end apart: 4, of which 3 were waited for; matrix products, arithmetic and copies ran while one was open for 0% of the time, Pallas kernels for 6%

profile of v2, /device:TPU:16, one launch (start us, length us, event | category | flops | bytes accessed | tf_op | source)
XLA Modules:
  0.0 98.2 jit_solution(13648018614499466418)
XLA Ops:
  0.6 0.1 pad_add_fusion.here
  0.7 0.9 copy-done
  1.6 0.9 copy-done.1
  2.5 0.8 turn.2
  3.4 0.1 collective-permute-start
  3.5 0.5 copy-done.5
  4.0 0.1 select_reduce_fusion
  4.1 0.1 rev.7
  4.2 0.7 copy-done.3
  4.8 0.1 rev.6
  4.9 0.1 copy.8
  5.0 0.7 pack.2
  5.7 2.2 %collective-permute-start.1 = (f32[2,15,8,128]{3,2,1,0:T(8,128)S(1)}, f32[2,15,8,128]{3,2,1,0:T(8,128)S(1)}, u32[]{:S(2)}, u32[]{:S(2)}) collective-permute-start(f32[2,15,8,128]{3,2,1,0:T(8,128)S(1)} %pack.2), channel_id=1, source_target_pairs={{0,1},{1,0},{2,3},{3,2},{4,5},{5,4},{6,7},{7,6},{8,9},{9,8},{10,11... | collective-permute-start | bytes 368648 | tf_op jit(solution)/shard_map/ppermute | solution.py:369
  7.9 0.1 broadcast_in_dim.2.base
  8.0 2.9 %propagate_rows.2 = (f32[32,8,128]{2,1,0:T(8,128)S(1)}, f32[15,8,128]{2,1,0:T(8,128)S(1)}, f32[44,8,128]{2,1,0:T(8,128)S(1)}, f32[15,8,128]{2,1,0:T(8,128)S(1)}, f32[32,8,128]{2,1,0:T(8,128)S(1)}) custom-call(s32[2]{0:T(128)S(1)} %pad_add_fusion.here, f32[4,8]{1,0:T(4,128)S(1)} %broadcast_select_fusion.1.mask, f32[8,8,128]{2,1,0:T(8,128)S(1)} %broadcast_in_dim.2.base, ...), custom_call_target="tpu_custom_call" | custom-call | flops 20000000 | bytes 4000000 | tf_op jit(solution)/shard_map/propagate_rows/pallas_call | solution.py:232
  10.9 1.6 %collective-permute-done.1.other = f32[2,15,8,128]{3,2,1,0:T(8,128)S(1)} collective-permute-done((f32[2,15,8,128]{3,2,1,0:T(8,128)S(1)}, f32[2,15,8,128]{3,2,1,0:T(8,128)S(1)}, u32[]{:S(2)}, u32[]{:S(2)}) %collective-permute-start.1) | collective-permute-done | bytes 122912 | tf_op jit(solution)/shard_map/ppermute | solution.py:369
  12.5 2.5 %propagate_band.2 = (f32[15,8,128]{2,1,0:T(8,128)S(1)}, f32[32,8,128]{2,1,0:T(8,128)S(1)}, f32[512,128]{1,0:T(8,128)S(1)}) custom-call(s32[2]{0:T(128)S(1)} %pad_add_fusion.here, f32[4,8]{1,0:T(4,128)S(1)} %broadcast_select_fusion.1.mask, f32[8,8,128]{2,1,0:T(8,128)S(1)} %broadcast_in_dim.2.base, f32[32,8,128]{2,1,0:T(8,128)S(1)} %get-tuple-element.22.end, ...), custom_call_target="tpu_custom_call" | custom-call | tf_op jit(solution)/shard_map/propagate_band/pallas_call | solution.py:300
  15.0 24.1 %all_to_all.20.both = f32[64,8,128]{2,1,0:T(8,128)S(1)} all-to-all(f32[64,8,128]{2,1,0:T(8,128)S(1)} %bitcast.17), channel_id=1, replica_groups=mesh['tm'=64,'sx'=2,'sy'=2] {'tm'}, dimensions={0} | all-to-all | bytes 524288 | tf_op jit(solution)/shard_map/all_to_all | solution.py:376
  39.1 0.3 cycle.2
  39.4 16.2 %all_to_all.21 = f32[64,4,128]{2,1,0:T(4,128)S(1)} all-to-all(f32[64,4,128]{2,1,0:T(4,128)S(1)} %cycle.2), channel_id=1, replica_groups=mesh['tm'=64,'sx'=2,'sy'=2] {'tm'}, dimensions={0} | all-to-all | bytes 262144 | tf_op jit(solution)/shard_map/all_to_all | solution.py:377
  55.5 0.7 turn.3
  56.2 0.1 collective-permute-start.2
  56.3 1.2 %collective-permute-done.2.halo.refs_1_ = f32[1,12,8,128]{3,2,1,0:T(8,128)S(1)} collective-permute-done((f32[1,12,8,128]{3,2,1,0:T(8,128)S(1)}, f32[1,12,8,128]{3,2,1,0:T(8,128)S(1)}, u32[]{:S(2)}, u32[]{:S(2)}) %collective-permute-start.2) | collective-permute-done | bytes 49184 | tf_op jit(solution)/shard_map/ppermute | solution.py:380
  57.5 0.7 pack.3
  58.2 0.7 collective-permute-start.3
  58.9 2.8 %propagate_rows.3 = (f32[32,8,128]{2,1,0:T(8,128)S(1)}, f32[15,8,128]{2,1,0:T(8,128)S(1)}) custom-call(s32[2]{0:T(128)S(1)} %pad_add_fusion.here, f32[4,8]{1,0:T(4,128)S(1)} %broadcast_select_fusion.1.mask, f32[8,8,128]{2,1,0:T(8,128)S(1)} %broadcast_in_dim.2.base, f32[32,8,128]{2,1,0:T(8,128)S(1)} %get-tuple-element.27.own.refs_0_, ...), custom_call_target="tpu_custom_call" | custom-call | flops 20000000 | bytes 4000000 | tf_op jit(solution)/shard_map/propagate_rows/pallas_call | solution.py:232
  61.7 2.3 %collective-permute-done.3.other = f32[1,15,8,128]{3,2,1,0:T(8,128)S(1)} collective-permute-done((f32[1,15,8,128]{3,2,1,0:T(8,128)S(1)}, f32[1,15,8,128]{3,2,1,0:T(8,128)S(1)}, u32[]{:S(2)}, u32[]{:S(2)}) %collective-permute-start.3) | collective-permute-done | bytes 61472 | tf_op jit(solution)/shard_map/ppermute | solution.py:382
  64.0 3.1 %propagate_band.3 = (f32[256,128]{1,0:T(8,128)S(1)}, f32[256,128]{1,0:T(8,128)}) custom-call(s32[2]{0:T(128)S(1)} %pad_add_fusion.here, f32[4,8]{1,0:T(4,128)S(1)} %broadcast_select_fusion.1.mask, f32[8,8,128]{2,1,0:T(8,128)S(1)} %broadcast_in_dim.2.base, f32[32,8,128]{2,1,0:T(8,128)S(1)} %get-tuple-element.30.end, ...), custom_call_target="tpu_custom_call" | custom-call | tf_op jit(solution)/shard_map/propagate_band/pallas_call | solution.py:300
  67.1 15.1 %all_to_all.22.offset = f32[64,4,128]{2,1,0:T(4,128)S(1)} all-to-all(f32[64,4,128]{2,1,0:T(4,128)S(1)} %bitcast.20), channel_id=1, replica_groups=mesh['tm'=64,'sx'=2,'sy'=2] {'tm'}, dimensions={0} | all-to-all | bytes 262144 | tf_op jit(solution)/shard_map/all_to_all | solution.py:387
  82.2 0.3 cycle.3
  82.5 15.1 %all_to_all.23 = f32[64,4,128]{2,1,0:T(4,128)S(1)} all-to-all(f32[64,4,128]{2,1,0:T(4,128)S(1)} %cycle.3), channel_id=1, replica_groups=mesh['tm'=64,'sx'=2,'sy'=2] {'tm'}, dimensions={0} | all-to-all | bytes 262144 | tf_op jit(solution)/shard_map/all_to_all | solution.py:388
  97.5 0.7 copy.10
  (12 shorter events, 0.0 us)
Async XLA Ops:
  0.7 0.9 copy-start
  1.6 0.9 copy-start.1
  2.5 0.9 copy-start.4
  3.3 0.7 copy-start.5
  3.4 1.7 %collective-permute-start = (f32[2,12,8,128]{3,2,1,0:T(8,128)S(1)}, f32[2,12,8,128]{3,2,1,0:T(8,128)S(1)}, u32[]{:S(2)}, u32[]{:S(2)}) collective-permute-start(f32[2,12,8,128]{3,2,1,0:T(8,128)S(1)} %get-tuple-element.20), channel_id=1, source_target_pairs={{0,2},{2,0},{1,3},{3,1},{4,6},{6,4},{5,7},{7,5},{8,10},{10,8},{9,1... | collective-permute-start | bytes 294920 | tf_op jit(solution)/shard_map/ppermute | solution.py:367
  4.2 0.7 copy-start.3
  5.0 2.9 %copy-start.2 = (f32[1,8,32,128]{3,2,1,0:T(8,128)S(1)}, f32[1,8,32,128]{3,2,1,0:T(8,128)}, u32[]{:S(2)}) copy-start(f32[1,8,32,128]{3,2,1,0:T(8,128)} %param.7) | copy-start | bytes 393220
  5.7 6.8 %collective-permute-start.1 = (f32[2,15,8,128]{3,2,1,0:T(8,128)S(1)}, f32[2,15,8,128]{3,2,1,0:T(8,128)S(1)}, u32[]{:S(2)}, u32[]{:S(2)}) collective-permute-start(f32[2,15,8,128]{3,2,1,0:T(8,128)S(1)} %pack.2), channel_id=1, source_target_pairs={{0,1},{1,0},{2,3},{3,2},{4,5},{5,4},{6,7},{7,6},{8,9},{9,8},{10,11... | collective-permute-start | bytes 368648 | tf_op jit(solution)/shard_map/ppermute | solution.py:369
  56.2 1.3 %collective-permute-start.2 = (f32[1,12,8,128]{3,2,1,0:T(8,128)S(1)}, f32[1,12,8,128]{3,2,1,0:T(8,128)S(1)}, u32[]{:S(2)}, u32[]{:S(2)}) collective-permute-start(f32[1,12,8,128]{3,2,1,0:T(8,128)S(1)} %get-tuple-element.28), channel_id=1, source_target_pairs={{0,2},{2,0},{1,3},{3,1},{4,6},{6,4},{5,7},{7,5},{8,10},{10,8},{9,1... | collective-permute-start | bytes 147464 | tf_op jit(solution)/shard_map/ppermute | solution.py:380
  58.2 5.8 %collective-permute-start.3 = (f32[1,15,8,128]{3,2,1,0:T(8,128)S(1)}, f32[1,15,8,128]{3,2,1,0:T(8,128)S(1)}, u32[]{:S(2)}, u32[]{:S(2)}) collective-permute-start(f32[1,15,8,128]{3,2,1,0:T(8,128)S(1)} %pack.3), channel_id=1, source_target_pairs={{0,1},{1,0},{2,3},{3,2},{4,5},{5,4},{6,7},{7,6},{8,9},{9,8},{10,11... | collective-permute-start | bytes 184328 | tf_op jit(solution)/shard_map/ppermute | solution.py:382

commit v3 on v0

v3 whole, which is shorter than its diff:
```python
import functools

import jax
import jax.numpy as jnp
from jax import lax
from jax.experimental import pallas as pl
from jax.experimental.pallas import tpu as pltpu
from jax.sharding import PartitionSpec as P

RB = 8
REGIONS = 4
FSTEPS = 4
SWEEPS = 3
ITERS = 2
cond_slope = 0.25
joule_slope = 0.3

HALO = FSTEPS * SWEEPS
ROWS = 32
LAYERS = 8
COLS = 128
BOX = ROWS + HALO
EDGE = 2 * HALO
WIDE = 64
PACK = 22
BLOCKS = 6
SENT = 9
FRINGE = 8
VMEM = pltpu.VMEM


def spec():
    return pl.BlockSpec(memory_space=VMEM)


def sspec():
    return pl.BlockSpec(memory_space=pltpu.SMEM)


def plane(*shape):
    return jax.ShapeDtypeStruct((*shape, LAYERS, COLS), jnp.float32)


def flat(rows):
    return jax.ShapeDtypeStruct((rows, COLS), jnp.float32)


def call(kernel, outs, scalars, arrays, name, work=(), cost=None, place=VMEM):
    single = not isinstance(outs, list)
    return pl.pallas_call(
        kernel,
        out_shape=outs,
        in_specs=[sspec()] * len(scalars) + [pl.BlockSpec(memory_space=place)] * len(arrays),
        out_specs=spec() if single else [spec()] * len(outs),
        scratch_shapes=list(work),
        cost_estimate=cost,
        compiler_params=pltpu.CompilerParams(vmem_limit_bytes=8 * 1024 * 1024),
        name=name,
    )(*scalars, *arrays)


def lanes():
    return lax.broadcasted_iota(jnp.int32, (LAYERS, COLS), 1)


def layers():
    return lax.broadcasted_iota(jnp.int32, (LAYERS, COLS), 0)


def moved(value, known, unknown=None):
    known = known % COLS
    if unknown is None:
        return pltpu.roll(value, known, 1) if known else value
    return pltpu.roll(value, (unknown + known) & (COLS - 1), 1)


def native_row(here, r):
    return jnp.where(here[0] == 0, r, ROWS - 1 - r)


def native(here, ref, r):
    return ref[pl.ds(native_row(here, r), LAYERS, stride=ROWS), :]


def box_row(here, own, far, r):
    return own[r] if r < ROWS else native(here, far, r - ROWS)


def load_kernel(here, *refs):
    arrays, outs, held, sem = refs[:3], refs[3:6], refs[6], refs[7]
    copies = [pltpu.make_async_copy(arrays[k], held.at[k], sem.at[k]) for k in range(3)]
    for copy in copies:
        copy.start()
    for k in range(3):
        copies[k].wait()
        for r in range(ROWS):
            outs[k][r] = native(here, held.at[k], r)


def banded(i, row):
    return jnp.where(lanes() < WIDE, moved(row(i), EDGE), moved(row(PACK + i), EDGE + WIDE))


class Part:
    def __init__(self, n, packed, power, base, heat, work):
        self.n, self.packed, self.power, self.base, self.heat = n, packed, power, base, heat
        self.state, self.tmp, self.wx, self.wyp, self.wzp, self.inv, self.rhs = work

    def prepare(self, m, now, old, coef_now, coef_old, half):
        n, packed = self.n, self.packed
        lane = lanes()
        layer = layers()
        edge = jnp.where(layer == 0, 1.0, 0.0)
        if not packed:
            edge = edge + jnp.where(lane == 0, 1.0, 0.0) + jnp.where(lane == COLS - 1, 1.0, 0.0)
        cond = []
        for r in range(n):
            cur = self.state[now, r]
            tanh = jnp.tanh(cur)
            cond.append((half * self.base(r)) * (1.0 - cond_slope * tanh))
            source = (half * self.heat(m, r)) * self.power[r] * (1.0 + joule_slope * tanh)
            self.rhs[r] = (coef_now * cur + coef_old * self.state[old, r]) + source
        faces = [None] * (n + 1)
        for r in range(1, n):
            faces[r] = cond[r - 1] + cond[r]
        if packed:
            faces[0] = jnp.where(lane < WIDE, 0.0, cond[0] + moved(cond[n - 1], WIDE))
            faces[n] = cond[n - 1] + moved(cond[0], WIDE)
        for r in range(n):
            c = cond[r]
            north = c + moved(c, -1)
            if not packed:
                north = jnp.where(lane == COLS - 1, 0.0, north)
            up = jnp.where(layer == LAYERS - 1, 0.0, 0.5 * (c + pltpu.roll(c, LAYERS - 1, 0)))
            total = (north + moved(north, 1)) + (up + pltpu.roll(up, 1, 0)) + (1.0 + edge * c)
            low = faces[r]
            if r == 0:
                low = c if low is None else low + jnp.where(lane < WIDE, c, 0.0)
            high = c if faces[r + 1] is None else faces[r + 1]
            self.wyp[r] = north
            self.wzp[r] = up
            self.inv[r] = 1.0 / (total + (low + high))
        for r in range(n + 1):
            if faces[r] is not None:
                self.wx[r] = faces[r]

    def sweep(self, source, store):
        n, packed = self.n, self.packed
        vs = [source(r) for r in range(n)]
        for r in range(n):
            v = vs[r]
            north = self.wyp[r]
            up = self.wzp[r]
            across = north * moved(v, -1) + moved(north * v, 1)
            along = up * pltpu.roll(v, LAYERS - 1, 0) + pltpu.roll(up * v, 1, 0)
            acc = self.rhs[r]
            if r:
                acc = acc + self.wx[r] * vs[r - 1]
            elif packed:
                acc = acc + self.wx[0] * moved(vs[n - 1], WIDE)
            if r < n - 1:
                acc = acc + self.wx[r + 1] * vs[r + 1]
            elif packed:
                acc = acc + self.wx[n] * moved(vs[0], WIDE)
            store(r, (acc + (across + along)) * self.inv[r])

    def relax(self, k, now, old):
        state, tmp = self.state, self.tmp

        def first(r, value):
            tmp[0, r] = value

        def second(r, value):
            tmp[1, r] = value

        def third(r, value):
            state[old, r] = value

        if k == 0:
            self.sweep(lambda r: state[now, r], first)
        elif k == 1:
            self.sweep(lambda r: tmp[0, r], second)
        else:
            self.sweep(lambda r: tmp[1, r], third)


def advance(*parts):
    def step(m, carry):
        start = m == 0
        now = lax.rem(m, 2)
        old = 1 - now
        coef_now = jnp.where(start, 1.0, 4.0 / 3.0).astype(jnp.float32)
        coef_old = jnp.where(start, 0.0, -1.0 / 3.0).astype(jnp.float32)
        half = jnp.where(start, 0.5, 1.0 / 3.0).astype(jnp.float32)
        for part in parts:
            part.prepare(m, now, old, coef_now, coef_old, half)
        for k in range(SWEEPS):
            for part in parts:
                part.relax(k, now, old)
        return carry

    lax.fori_loop(0, FSTEPS, step, 0)


def work_of(n):
    return [VMEM((2, n, LAYERS, COLS), jnp.float32)] * 2 + [VMEM((n + 1, LAYERS, COLS), jnp.float32)] * 5


def turned(here, block):
    return jnp.where(here[0] == 0, block, 7 - block)


def mask_of(here, mask):
    return lambda m, block: mask[m, turned(here, block)].astype(jnp.float32)


def tile_part(here, mask, base, power, work):
    on = mask_of(here, mask)
    return Part(BOX, False, power, lambda r: base[r // RB], lambda m, r: on(m, r // RB), work)


def band_part(here, mask, base, power, work):
    on = mask_of(here, mask)
    low = lanes() < WIDE

    def two(value):
        return lambda i: jnp.where(low, value(i // RB), value((i + PACK) // RB))

    return Part(PACK, True, power, two(lambda b: base[b]), lambda m, i: two(lambda b: on(m, b))(i), work)


def pack_kernel(here, own, far, power_own, power_far, rate, out):
    left = here[1] == 0
    lane = lanes()
    edge = jnp.where(left, EDGE, 0)
    fringe = jnp.where(left, HALO, 0)
    for k, (near, other) in enumerate(((own, far), (power_own, power_far))):
        for i in range(SENT):
            value = None
            for q in range(5):
                r = min(q * SENT + i, BOX - 1)
                part = moved(box_row(here, near, other, r), q * EDGE, edge)
                value = part if value is None else jnp.where(lane < q * EDGE, value, part)
            out[k * SENT + i] = value
    for j in range(FRINGE):
        value = None
        for g in range(4):
            part = moved(rate[g * FRINGE + j], g * 32, fringe)
            value = part if value is None else jnp.where(lane < g * 32, value, part)
        out[2 * SENT + j] = jnp.where((lane & 31) < HALO, value, 0.0)


def tile_kernel(here, mask, ids, conductivity, own, far, power_own, power_far, *refs):
    end, base, power, band, power_band, *work = refs
    state = work[0]
    layer = layers()
    for b in range(BLOCKS):
        value = jnp.zeros((LAYERS, COLS), jnp.float32)
        for l in range(LAYERS):
            value = jnp.where(layer == l, conductivity[ids[l, turned(here, b)]], value)
        base[b] = value
    for r in range(BOX):
        row = box_row(here, own, far, r)
        state[0, r] = row
        state[1, r] = row
        power[r] = box_row(here, power_own, power_far, r)
    for i in range(PACK):
        band[i] = banded(i, lambda r: state[0, r])
        power_band[i] = banded(i, lambda r: power[r])
    advance(tile_part(here, mask, base, power, work))
    for r in range(ROWS):
        end[r] = state[0, r]


def fringe_shift(left):
    return jnp.where(left, EDGE, HALO)


def merged(here, r, state, end):
    lane = lanes()
    left = here[1] == 0
    border = ((lane >= COLS - HALO) & left) | ((lane < HALO) & jnp.logical_not(left))
    return jnp.where(border, moved(state[0, r % PACK], -EDGE - WIDE * (r // PACK)), end)


def band_kernel(here, mask, end, start, rate, base, band, power_own, other, *refs):
    power, offset_out, send, first_band, *work = refs
    state = work[0]
    lane = lanes()
    left = here[1] == 0
    mine = ((lane & (WIDE - 1)) < EDGE) == left
    place = jnp.where(left, EDGE, 0)

    def received(k, i):
        parts = []
        for g in range(2):
            r = g * PACK + i
            parts.append(moved(other[k * SENT + r % SENT], g * WIDE - EDGE * (r // SENT), place))
        return jnp.where(lane < WIDE, parts[0], parts[1])

    for i in range(PACK):
        row = jnp.where(mine, band[i], received(0, i))
        state[0, i] = row
        state[1, i] = row
        first_band[i] = row
        power[i] = jnp.where(mine, power_own[i], received(1, i))
    advance(band_part(here, mask, base, power, work))
    for r in range(ROWS):
        d = rate[r]
        offset = merged(here, r, state, end[r]) - d * start[r]
        offset_out[r] = offset
        x = native_row(here, r)
        at = lax.div(x, 4) * 10 + lax.rem(x, 4)
        send[pl.ds(at, LAYERS, stride=80), :] = d
        send[pl.ds(at + 5, LAYERS, stride=80), :] = offset
    back = COLS - fringe_shift(left)
    for j in range(FRINGE):
        first, last = None, None
        for g in range(4):
            r = g * FRINGE + j
            by = g * 32 - WIDE * (r // PACK)
            u = moved(first_band[r % PACK], by, back)
            f = moved(state[0, r % PACK], by, back)
            first = u if g == 0 else jnp.where(lane < g * 32, first, u)
            last = f if g == 0 else jnp.where(lane < g * 32, last, f)
        d = other[2 * SENT + j]
        send[pl.ds(j * 80 + 4, LAYERS, stride=10), :] = d
        send[pl.ds(j * 80 + 9, LAYERS, stride=10), :] = last - d * first


def turn_kernel(here, states, out, send):
    for r in range(ROWS):
        x = native_row(here, r)
        row = states[pl.ds(lax.div(x, 4) * 5 + lax.rem(x, 4), LAYERS, stride=40), :]
        out[r] = row
        if r >= ROWS - HALO:
            send[r - (ROWS - HALO)] = row
    for j in range(FRINGE):
        row = states[pl.ds(j * 40 + 4, LAYERS, stride=5), :]
        out[ROWS + j] = row
        send[HALO + j] = row


def later_kernel(here, mask, own, far, rate, base, power, power_band, offset_before, *refs):
    send, jump, *work = refs
    tile, band = work[:7], work[7:]
    lane = lanes()
    slot = lane & (WIDE - 1)
    left = here[1] == 0
    shift = fringe_shift(left)
    fringe = (slot >= shift) & (slot < shift + HALO)
    for r in range(BOX):
        row = own[r] if r < ROWS else far[BOX - 1 - r]
        tile[0][0, r] = row
        tile[0][1, r] = row
    for i in range(PACK):
        parts = []
        for g in range(2):
            r = g * PACK + i
            source, k, at = (own, r, ROWS) if r < ROWS else (far, 2 * ROWS - 1 - r, HALO)
            parts.append(moved(source[at + k % FRINGE], g * WIDE - 32 * (k // FRINGE), shift))
        beside = jnp.where(lane < WIDE, parts[0], parts[1])
        row = jnp.where(fringe, beside, banded(i, lambda r: tile[0][0, r]))
        band[0][0, i] = row
        band[0][1, i] = row
    advance(
        tile_part(here, mask, base, power, tile),
        band_part(here, mask, base, power_band, band),
    )
    for r in range(ROWS):
        f = merged(here, r, band[0], tile[0][0, r])
        du = rate[r] * own[r]
        x = native_row(here, r)
        send[pl.ds(x, LAYERS, stride=ROWS), :] = f - du
        jump[pl.ds(x, LAYERS, stride=ROWS), :] = f - (du + offset_before[r])


def solve(slabs, rate, offset, store):
    scale = rate(0)
    shift = offset(0)
    for k in range(1, slabs):
        d = rate(k)
        scale = scale * d
        shift = d * shift + offset(k)
    u = shift / (1.0 - scale)
    store(0, u)
    for k in range(slabs - 1):
        u = rate(k) * u + offset(k)
        store(k + 1, u)


def cycle_kernel(slabs, both, out):
    def store(k, u):
        out[5 * k:5 * k + 5] = u

    solve(slabs, lambda k: both[10 * k:10 * k + 5], lambda k: both[10 * k + 5:10 * k + 10], store)


def cycle_later_kernel(slabs, both, offset, out):
    def store(k, u):
        out[k] = u

    solve(slabs, lambda k: both[10 * k:10 * k + 4], lambda k: offset[k], store)


SWAP = [(0, 1), (1, 0)]


def spread(x, slabs):
    x = x.reshape(slabs, x.shape[0] // slabs, 1, COLS)
    return lax.all_to_all(x, "tm", 0, 0, tiled=True).reshape(-1, COLS)


def shards(initial_states, coarse_decay, power_map, power_mask, region_ids, region_conductivity):
    slabs = lax.axis_size("tm")
    here = jnp.stack([lax.axis_index("sx"), lax.axis_index("sy")]).astype(jnp.int32)
    states, powers, decay = (
        x.reshape(LAYERS * ROWS, COLS) for x in (initial_states, power_map, coarse_decay)
    )
    mask = power_mask[0]

    far = lax.ppermute(states, "sx", SWAP)
    power_far = lax.ppermute(powers, "sx", SWAP)
    start, power_own, rate = call(
        load_kernel,
        [plane(ROWS)] * 3,
        [here],
        [pltpu.with_memory_space_constraint(x, pltpu.HBM) for x in (states, powers, decay)],
        "load",
        [VMEM((3, LAYERS * ROWS, COLS), jnp.float32), pltpu.SemaphoreType.DMA((3,))],
        pl.CostEstimate(flops=2_000_000, bytes_accessed=800_000, transcendentals=0),
        pltpu.HBM,
    )
    sent = call(pack_kernel, plane(2 * SENT + FRINGE), [here], [start, far, power_own, power_far, rate], "pack")
    other = lax.ppermute(sent, "sy", SWAP)
    end, base, power, band, power_band = call(
        tile_kernel,
        [plane(n) for n in (ROWS, BLOCKS, BOX, PACK, PACK)],
        [here, mask, region_ids, region_conductivity],
        [start, far, power_own, power_far],
        "propagate_tile",
        work_of(BOX),
        pl.CostEstimate(flops=20_000_000, bytes_accessed=4_000_000, transcendentals=400_000),
    )
    power_band, offset, both = call(
        band_kernel,
        [plane(PACK), plane(ROWS), flat(640)],
        [here, mask],
        [end, start, rate, base, band, power_band, other],
        "propagate_band",
        [VMEM((PACK, LAYERS, COLS), jnp.float32)] + work_of(PACK),
    )
    both = spread(both, slabs)
    states = spread(call(functools.partial(cycle_kernel, slabs), flat(320), [], [both], "cycle"), slabs)

    own, send = call(turn_kernel, [plane(ROWS + FRINGE), plane(HALO + FRINGE)], [here], [states], "turn")
    far = lax.ppermute(send, "sx", SWAP)
    later, jump = call(
        later_kernel,
        [flat(256), flat(256)],
        [here, mask],
        [own, far, rate, base, power, power_band, offset],
        "propagate_later",
        work_of(BOX) + work_of(PACK),
    )
    later = lax.all_to_all(later.reshape(slabs, 4, COLS), "tm", 0, 0, tiled=True)
    states = call(
        functools.partial(cycle_later_kernel, slabs),
        jax.ShapeDtypeStruct((slabs, 4, COLS), jnp.float32), [], [both, later], "cycle_later",
    )
    states = lax.all_to_all(states, "tm", 0, 0, tiled=True)
    shape = (1, LAYERS, ROWS, COLS)
    return states.reshape(shape), jump.reshape(shape)


def solution(mesh):
    return jax.shard_map(
        shards,
        mesh=mesh,
        in_specs=(
            P("tm", None, "sx", "sy"),
            P("tm", None, "sx", "sy"),
            P(None, "sx", "sy"),
            P("tm", None, None),
            P(),
            P(),
        ),
        out_specs=(P("tm", None, "sx", "sy"), P("tm", None, "sx", "sy")),
        check_vma=False,
    )
```

time: 2390 us -> 94.1 us (0.04)
  waiting for transfers between devices: 1960 us -> 2.68 us
  starting transfers between devices: 246 us -> 2.84 us
  other arithmetic: 163 us -> 0.07 us
  blocking collectives: 0 us -> 72.6 us
    psum x2 -> x0, waiting for transfers between devices: 1090 us -> none  [broadcast(): return lax.psum(jnp.where(mine, x, jnp.zeros_like(x)), axis)]
    all_gather x3 -> x0, waiting for transfers between devices: 685 us -> none  [entering(): everything = jax.tree.map(lambda part: lax.all_gather(part, axis), x)]
    ppermute x97 -> x4, starting transfers between devices: 246 us -> 2.84 us  [the longest x1 2.16 us: shards(): other = lax.ppermute(sent, 'sy', SWAP)]
    ppermute x97 -> x4, waiting for transfers between devices: 180 us -> 2.68 us  [the longest x1 1.41 us: shards(): other = lax.ppermute(sent, 'sy', SWAP)]
    select_n x130 -> x0, other arithmetic: 141 us -> none  [the longest x128 138 us: step(): return jax.tree.map(lambda a, b: jnp.where(reached, a, b), new, before)]
    all_to_all x0 -> x4, blocking collectives: none -> 72.6 us  [the longest x2 42 us: spread(): return lax.all_to_all(x, 'tm', 0, 0, tiled=True).reshape(-1, COLS)]
  transfers between devices with their start and end apart: 102 -> 4, of which waited for: 73 -> 2; matrix products, arithmetic and copies ran while one was open for 1% -> 0% of each run, Pallas kernels for 0% -> 5%
where the time goes in v3:
time: 94.1 us; the launch traced here: 93.9 us
  blocking collectives  72.6 us (77%)
  Pallas kernels  14.3 us (15%)
  starting transfers between devices  2.84 us (3%)
  waiting for transfers between devices  2.68 us (3%)
    all_to_all x2, blocking collectives, spread(): return lax.all_to_all(x, 'tm', 0, 0, tiled=True).reshape(-1, COLS)  42 us
    all_to_all x1, blocking collectives, shards(): lax.all_to_all(later.reshape(slabs, 4, COLS), 'tm', 0, 0, tiled=True)  15.4 us
    all_to_all x1, blocking collectives, shards(): states = lax.all_to_all(states, 'tm', 0, 0, tiled=True)  15.2 us
    pallas_call x8, Pallas kernels, call(): pl.pallas_call(kernel, out_shape=outs, in_specs=[sspec()] * len(scalars)...  14.3 us
    ppermute x1, starting transfers between devices, shards(): other = lax.ppermute(sent, 'sy', SWAP)  2.16 us
  transfers between devices with their start and end apart: 4, of which 2 were waited for; matrix products, arithmetic and copies ran while one was open for 0% of the time, Pallas kernels for 5%

profile of v3, /device:TPU:16, one launch (start us, length us, event | category | flops | bytes accessed | tf_op | source)
XLA Modules:
  0.0 93.9 jit_solution(96797330691072863)
XLA Ops:
  0.6 0.1 collective-permute-start
  0.7 0.5 collective-permute-start.1
  1.2 0.1 pad_add_fusion.here
  1.3 1.9 %load.1 = (f32[32,8,128]{2,1,0:T(8,128)S(1)}, f32[32,8,128]{2,1,0:T(8,128)S(1)}, f32[32,8,128]{2,1,0:T(8,128)S(1)}) custom-call(s32[2]{0:T(128)S(1)} %pad_add_fusion.here, f32[256,128]{1,0:T(8,128)} %bitcast.25, f32[256,128]{1,0:T(8,128)} %bitcast.27, f32[256,128]{1,0:T(8,128)} %bitcast.23), custom_call_target="tpu_custom_call" | custom-call | flops 2000000 | bytes 800000 | tf_op jit(solution)/shard_map/load/pallas_call | solution.py:50
  3.2 0.0 collective-permute-done.far
  3.2 0.0 collective-permute-done.1.power_far
  3.2 0.0 copy-start
  3.2 0.0 copy-start.1
  3.2 0.8 pack.1
  4.0 0.0 copy-start.2
  4.0 2.2 %collective-permute-start.2 = (f32[26,8,128]{2,1,0:T(8,128)S(1)}, f32[26,8,128]{2,1,0:T(8,128)S(1)}, u32[]{:S(2)}, u32[]{:S(2)}) collective-permute-start(f32[26,8,128]{2,1,0:T(8,128)S(1)} %pack.1), channel_id=1, source_target_pairs={{0,1},{1,0},{2,3},{3,2},{4,5},{5,4},{6,7},{7,6},{8,9},{9,8},{10,11... | collective-permute-start | bytes 319496 | tf_op jit(solution)/shard_map/ppermute | solution.py:435
  6.2 0.0 copy-done
  6.2 0.0 copy-done.1
  6.2 0.0 copy-done.2
  6.2 3.0 %propagate_tile.1 = (f32[32,8,128]{2,1,0:T(8,128)S(1)}, f32[6,8,128]{2,1,0:T(8,128)S(1)}, f32[44,8,128]{2,1,0:T(8,128)S(1)}, f32[22,8,128]{2,1,0:T(8,128)S(1)}, f32[22,8,128]{2,1,0:T(8,128)S(1)}) custom-call(s32[2]{0:T(128)S(1)} %pad_add_fusion.here, s32[4,8]{1,0:T(4,128)S(1)} %bitcast.19, s32[8,8]{1,0:T(8,128)S(1)} %copy-done.1, f32[4]{0:T(128)S(1)} %copy-done.2, ...), custom_call_target="tpu_custom_call" | custom-call | flops 20000000 | bytes 4000000 | tf_op jit(solution)/shard_map/propagate_tile/pallas_call | solution.py:50
  9.2 1.4 %collective-permute-done.2.other = f32[26,8,128]{2,1,0:T(8,128)S(1)} collective-permute-done((f32[26,8,128]{2,1,0:T(8,128)S(1)}, f32[26,8,128]{2,1,0:T(8,128)S(1)}, u32[]{:S(2)}, u32[]{:S(2)}) %collective-permute-start.2) | collective-permute-done | bytes 106528 | tf_op jit(solution)/shard_map/ppermute | solution.py:435
  10.6 2.7 %propagate_band.1 = (f32[22,8,128]{2,1,0:T(8,128)S(1)}, f32[32,8,128]{2,1,0:T(8,128)S(1)}, f32[640,128]{1,0:T(8,128)S(1)}) custom-call(s32[2]{0:T(128)S(1)} %pad_add_fusion.here, s32[4,8]{1,0:T(4,128)S(1)} %bitcast.20, f32[32,8,128]{2,1,0:T(8,128)S(1)} %get-tuple-element.19.end, f32[32,8,128]{2,1,0:T(8,128)S(1)} %get-tuple-element.17.own.start, ...), custom_call_target="tpu_custom_call" | custom-call | tf_op jit(solution)/shard_map/propagate_band/pallas_call | solution.py:50
  13.3 25.4 %all_to_all.20 = f32[64,10,1,128]{3,2,1,0:T(1,128)S(1)} all-to-all(f32[64,10,1,128]{3,2,1,0:T(1,128)S(1)} %bitcast.17), channel_id=1, replica_groups=mesh['tm'=64,'sx'=2,'sy'=2] {'tm'}, dimensions={0} | all-to-all | bytes 655360 | tf_op jit(solution)/shard_map/all_to_all | solution.py:411
  38.7 0.3 cycle.1
  39.0 16.5 %all_to_all.21 = f32[64,5,1,128]{3,2,1,0:T(1,128)S(1)} all-to-all(f32[64,5,1,128]{3,2,1,0:T(1,128)S(1)} %bitcast.16), channel_id=1, replica_groups=mesh['tm'=64,'sx'=2,'sy'=2] {'tm'}, dimensions={0} | all-to-all | bytes 327680 | tf_op jit(solution)/shard_map/all_to_all | solution.py:411
  55.5 0.6 turn.1
  56.2 0.1 collective-permute-start.3
  56.3 1.3 %collective-permute-done.3.far = f32[20,8,128]{2,1,0:T(8,128)S(1)} collective-permute-done((f32[20,8,128]{2,1,0:T(8,128)S(1)}, f32[20,8,128]{2,1,0:T(8,128)S(1)}, u32[]{:S(2)}, u32[]{:S(2)}) %collective-permute-start.3) | collective-permute-done | bytes 81952 | tf_op jit(solution)/shard_map/ppermute | solution.py:457
  57.6 4.7 %propagate_later.1 = (f32[256,128]{1,0:T(8,128)S(1)}, f32[256,128]{1,0:T(8,128)}) custom-call(s32[2]{0:T(128)S(1)} %pad_add_fusion.here, s32[4,8]{1,0:T(4,128)S(1)} %bitcast.21, f32[40,8,128]{2,1,0:T(8,128)S(1)} %get-tuple-element.25.own, f32[20,8,128]{2,1,0:T(8,128)S(1)} %collective-permute-done.3.far, f32[32,8,128]{2,1,0:T(8,128)S(1)} %get-tuple-element.20.rate, ...), custom_call_target="tpu_custom_call" | custom-call | tf_op jit(solution)/shard_map/propagate_later/pallas_call | solution.py:50
  62.3 15.4 %all_to_all.22.offset = f32[64,4,128]{2,1,0:T(4,128)S(1)} all-to-all(f32[64,4,128]{2,1,0:T(4,128)S(1)} %bitcast.18), channel_id=1, replica_groups=mesh['tm'=64,'sx'=2,'sy'=2] {'tm'}, dimensions={0} | all-to-all | bytes 262144 | tf_op jit(solution)/shard_map/all_to_all | solution.py:466
  77.8 0.3 cycle_later.1
  78.0 15.2 %all_to_all.23 = f32[64,4,128]{2,1,0:T(4,128)S(1)} all-to-all(f32[64,4,128]{2,1,0:T(4,128)S(1)} %cycle_later.1), channel_id=1, replica_groups=mesh['tm'=64,'sx'=2,'sy'=2] {'tm'}, dimensions={0} | all-to-all | bytes 262144 | tf_op jit(solution)/shard_map/all_to_all | solution.py:471
  93.2 0.7 copy.11
Async XLA Ops:
  0.6 2.6 %collective-permute-start = (f32[256,128]{1,0:T(8,128)}, f32[256,128]{1,0:T(8,128)S(1)}, u32[]{:S(2)}, u32[]{:S(2)}) collective-permute-start(f32[256,128]{1,0:T(8,128)} %bitcast.24), channel_id=1, source_target_pairs={{0,2},{2,0},{1,3},{3,1},{4,6},{6,4},{5,7},{7,5},{8,10},{10,8},{9,1... | collective-permute-start | bytes 393224 | tf_op jit(solution)/shard_map/ppermute | solution.py:422
  0.7 2.5 %collective-permute-start.1 = (f32[256,128]{1,0:T(8,128)}, f32[256,128]{1,0:T(8,128)S(1)}, u32[]{:S(2)}, u32[]{:S(2)}) collective-permute-start(f32[256,128]{1,0:T(8,128)} %bitcast.26), channel_id=1, source_target_pairs={{0,2},{2,0},{1,3},{3,1},{4,6},{6,4},{5,7},{7,5},{8,10},{10,8},{9,1... | collective-permute-start | bytes 393224 | tf_op jit(solution)/shard_map/ppermute | solution.py:423
  3.2 3.0 %copy-start = (s32[1,4,8]{2,1,0:T(4,128)S(1)}, s32[1,4,8]{2,1,0:T(4,128)}, u32[]{:S(2)}) copy-start(s32[1,4,8]{2,1,0:T(4,128)} %param.9) | copy-start | bytes 388
  3.2 3.0 %copy-start.1 = (s32[8,8]{1,0:T(8,128)S(1)}, s32[8,8]{1,0:T(8,128)}, u32[]{:S(2)}) copy-start(s32[8,8]{1,0:T(8,128)} %ids.1) | copy-start | bytes 772
  4.0 2.2 %copy-start.2 = (f32[4]{0:T(128)S(1)}, f32[4]{0:T(128)}, u32[]{:S(2)}) copy-start(f32[4]{0:T(128)} %conductivity.1) | copy-start | bytes 52
  4.0 6.6 %collective-permute-start.2 = (f32[26,8,128]{2,1,0:T(8,128)S(1)}, f32[26,8,128]{2,1,0:T(8,128)S(1)}, u32[]{:S(2)}, u32[]{:S(2)}) collective-permute-start(f32[26,8,128]{2,1,0:T(8,128)S(1)} %pack.1), channel_id=1, source_target_pairs={{0,1},{1,0},{2,3},{3,2},{4,5},{5,4},{6,7},{7,6},{8,9},{9,8},{10,11... | collective-permute-start | bytes 319496 | tf_op jit(solution)/shard_map/ppermute | solution.py:435
  56.2 1.4 %collective-permute-start.3 = (f32[20,8,128]{2,1,0:T(8,128)S(1)}, f32[20,8,128]{2,1,0:T(8,128)S(1)}, u32[]{:S(2)}, u32[]{:S(2)}) collective-permute-start(f32[20,8,128]{2,1,0:T(8,128)S(1)} %get-tuple-element.26), channel_id=1, source_target_pairs={{0,2},{2,0},{1,3},{3,1},{4,6},{6,4},{5,7},{7,5},{8,10},{10,8},{9,1... | collective-permute-start | bytes 245768 | tf_op jit(solution)/shard_map/ppermute | solution.py:457

commit v4 on v3

--- a/solution.py
+++ b/solution.py
@@ -25,6 +25,7 @@
 PACK = 22
 BLOCKS = 6
 SENT = 9
+THIN = 4
 FRINGE = 8
 VMEM = pltpu.VMEM
 
@@ -74,6 +75,10 @@
     return pltpu.roll(value, (unknown + known) & (COLS - 1), 1)
 
 
+def position():
+    return lax.axis_index("sx"), lax.axis_index("sy")
+
+
 def native_row(here, r):
     return jnp.where(here[0] == 0, r, ROWS - 1 - r)
 
@@ -82,11 +87,17 @@
     return ref[pl.ds(native_row(here, r), LAYERS, stride=ROWS), :]
 
 
+def place_of(here, r, size):
+    up, down = (x // 4 * size + x % 4 for x in (r, ROWS - 1 - r))
+    return jnp.where(here[0] == 0, up, down)
+
+
 def box_row(here, own, far, r):
     return own[r] if r < ROWS else native(here, far, r - ROWS)
 
 
-def load_kernel(here, *refs):
+def load_kernel(*refs):
+    here = position()
     arrays, outs, held, sem = refs[:3], refs[3:6], refs[6], refs[7]
     copies = [pltpu.make_async_copy(arrays[k], held.at[k], sem.at[k]) for k in range(3)]
     for copy in copies:
@@ -104,7 +115,7 @@
 class Part:
     def __init__(self, n, packed, power, base, heat, work):
         self.n, self.packed, self.power, self.base, self.heat = n, packed, power, base, heat
-        self.state, self.tmp, self.wx, self.wyp, self.wzp, self.inv, self.rhs = work
+        self.state, self.wx, self.wyp, self.wzp, self.inv, self.rhs = work
 
     def prepare(self, m, now, old, coef_now, coef_old, half):
         n, packed = self.n, self.packed
@@ -144,9 +155,9 @@
             if faces[r] is not None:
                 self.wx[r] = faces[r]
 
-    def sweep(self, source, store):
+    def sweep(self, vs):
         n, packed = self.n, self.packed
-        vs = [source(r) for r in range(n)]
+        out = []
         for r in range(n):
             v = vs[r]
             north = self.wyp[r]
@@ -162,74 +173,54 @@
                 acc = acc + self.wx[r + 1] * vs[r + 1]
             elif packed:
                 acc = acc + self.wx[n] * moved(vs[0], WIDE)
-            store(r, (acc + (across + along)) * self.inv[r])
-
-    def relax(self, k, now, old):
-        state, tmp = self.state, self.tmp
-
-        def first(r, value):
-            tmp[0, r] = value
-
-        def second(r, value):
-            tmp[1, r] = value
-
-        def third(r, value):
-            state[old, r] = value
-
-        if k == 0:
-            self.sweep(lambda r: state[now, r], first)
-        elif k == 1:
-            self.sweep(lambda r: tmp[0, r], second)
-        else:
-            self.sweep(lambda r: tmp[1, r], third)
+            out.append((acc + (across + along)) * self.inv[r])
+        return out
 
 
 def advance(*parts):
-    def step(m, carry):
-        start = m == 0
-        now = lax.rem(m, 2)
-        old = 1 - now
-        coef_now = jnp.where(start, 1.0, 4.0 / 3.0).astype(jnp.float32)
-        coef_old = jnp.where(start, 0.0, -1.0 / 3.0).astype(jnp.float32)
-        half = jnp.where(start, 0.5, 1.0 / 3.0).astype(jnp.float32)
-        for part in parts:
-            part.prepare(m, now, old, coef_now, coef_old, half)
-        for k in range(SWEEPS):
+    def turn(t, carry):
+        for now in range(2):
+            old = 1 - now
+            start = (t == 0) if now == 0 else False
+            coef_now = jnp.where(start, 1.0, 4.0 / 3.0).astype(jnp.float32)
+            coef_old = jnp.where(start, 0.0, -1.0 / 3.0).astype(jnp.float32)
+            half = jnp.where(start, 0.5, 1.0 / 3.0).astype(jnp.float32)
             for part in parts:
-                part.relax(k, now, old)
+                part.prepare(2 * t + now, now, old, coef_now, coef_old, half)
+            values = [[part.state[now, r] for r in range(part.n)] for part in parts]
+            for k in range(SWEEPS):
+                values = [part.sweep(vs) for part, vs in zip(parts, values)]
+            for part, vs in zip(parts, values):
+                for r in range(part.n):
+                    part.state[old, r] = vs[r]
         return carry
 
-    lax.fori_loop(0, FSTEPS, step, 0)
+    lax.fori_loop(0, FSTEPS // 2, turn, 0)
 
 
 def work_of(n):
-    return [VMEM((2, n, LAYERS, COLS), jnp.float32)] * 2 + [VMEM((n + 1, LAYERS, COLS), jnp.float32)] * 5
+    return [VMEM((2, n, LAYERS, COLS), jnp.float32)] + [VMEM((n + 1, LAYERS, COLS), jnp.float32)] * 5
 
 
 def turned(here, block):
     return jnp.where(here[0] == 0, block, 7 - block)
 
 
-def mask_of(here, mask):
-    return lambda m, block: mask[m, turned(here, block)].astype(jnp.float32)
-
-
-def tile_part(here, mask, base, power, work):
-    on = mask_of(here, mask)
-    return Part(BOX, False, power, lambda r: base[r // RB], lambda m, r: on(m, r // RB), work)
-
-
-def band_part(here, mask, base, power, work):
-    on = mask_of(here, mask)
+def tile_part(base, heat, power, work):
+    return Part(BOX, False, power, lambda r: base[r // RB], lambda m, r: heat[m * BLOCKS + r // RB], work)
+
+
+def band_part(base, heat, power, work):
     low = lanes() < WIDE
 
-    def two(value):
-        return lambda i: jnp.where(low, value(i // RB), value((i + PACK) // RB))
-
-    return Part(PACK, True, power, two(lambda b: base[b]), lambda m, i: two(lambda b: on(m, b))(i), work)
-
-
-def pack_kernel(here, own, far, power_own, power_far, rate, out):
+    def two(ref, first, i):
+        return jnp.where(low, ref[first + i // RB], ref[first + (i + PACK) // RB])
+
+    return Part(PACK, True, power, lambda i: two(base, 0, i), lambda m, i: two(heat, m * BLOCKS, i), work)
+
+
+def pack_kernel(own, far, power_own, power_far, rate, out):
+    here = position()
     left = here[1] == 0
     lane = lanes()
     edge = jnp.where(left, EDGE, 0)
@@ -242,16 +233,17 @@
                 part = moved(box_row(here, near, other, r), q * EDGE, edge)
                 value = part if value is None else jnp.where(lane < q * EDGE, value, part)
             out[k * SENT + i] = value
-    for j in range(FRINGE):
+    for i in range(THIN):
         value = None
-        for g in range(4):
-            part = moved(rate[g * FRINGE + j], g * 32, fringe)
-            value = part if value is None else jnp.where(lane < g * 32, value, part)
-        out[2 * SENT + j] = jnp.where((lane & 31) < HALO, value, 0.0)
-
-
-def tile_kernel(here, mask, ids, conductivity, own, far, power_own, power_far, *refs):
-    end, base, power, band, power_band, *work = refs
+        for q in range(8):
+            part = moved(rate[q * THIN + i], q * 16, fringe)
+            value = part if value is None else jnp.where(lane < q * 16, value, part)
+        out[2 * SENT + i] = value
+
+
+def tile_kernel(mask, ids, conductivity, own, far, power_own, power_far, *refs):
+    here = position()
+    end, base, heat, power, band, power_band, *work = refs
     state = work[0]
     layer = layers()
     for b in range(BLOCKS):
@@ -259,6 +251,9 @@
         for l in range(LAYERS):
             value = jnp.where(layer == l, conductivity[ids[l, turned(here, b)]], value)
         base[b] = value
+        for m in range(FSTEPS):
+            on = mask[m, turned(here, b)].astype(jnp.float32)
+            heat[m * BLOCKS + b] = jnp.full((LAYERS, COLS), on, jnp.float32)
     for r in range(BOX):
         row = box_row(here, own, far, r)
         state[0, r] = row
@@ -267,7 +262,7 @@
     for i in range(PACK):
         band[i] = banded(i, lambda r: state[0, r])
         power_band[i] = banded(i, lambda r: power[r])
-    advance(tile_part(here, mask, base, power, work))
+    advance(tile_part(base, heat, power, work))
     for r in range(ROWS):
         end[r] = state[0, r]
 
@@ -283,7 +278,8 @@
     return jnp.where(border, moved(state[0, r % PACK], -EDGE - WIDE * (r // PACK)), end)
 
 
-def band_kernel(here, mask, end, start, rate, base, band, power_own, other, *refs):
+def band_kernel(end, start, rate, base, heat, band, power_own, other, *refs):
+    here = position()
     power, offset_out, send, first_band, *work = refs
     state = work[0]
     lane = lanes()
@@ -304,13 +300,12 @@
         state[1, i] = row
         first_band[i] = row
         power[i] = jnp.where(mine, power_own[i], received(1, i))
-    advance(band_part(here, mask, base, power, work))
+    advance(band_part(base, heat, power, work))
     for r in range(ROWS):
         d = rate[r]
         offset = merged(here, r, state, end[r]) - d * start[r]
         offset_out[r] = offset
-        x = native_row(here, r)
-        at = lax.div(x, 4) * 10 + lax.rem(x, 4)
+        at = place_of(here, r, 10)
         send[pl.ds(at, LAYERS, stride=80), :] = d
         send[pl.ds(at + 5, LAYERS, stride=80), :] = offset
     back = COLS - fringe_shift(left)
@@ -323,15 +318,16 @@
             f = moved(state[0, r % PACK], by, back)
             first = u if g == 0 else jnp.where(lane < g * 32, first, u)
             last = f if g == 0 else jnp.where(lane < g * 32, last, f)
-        d = other[2 * SENT + j]
+        d = moved(other[2 * SENT + j % THIN], -16 * (j // THIN))
+        d = jnp.where((lane & 31) < HALO, d, 0.0)
         send[pl.ds(j * 80 + 4, LAYERS, stride=10), :] = d
         send[pl.ds(j * 80 + 9, LAYERS, stride=10), :] = last - d * first
 
 
-def turn_kernel(here, states, out, send):
+def turn_kernel(states, out, send):
+    here = position()
     for r in range(ROWS):
-        x = native_row(here, r)
-        row = states[pl.ds(lax.div(x, 4) * 5 + lax.rem(x, 4), LAYERS, stride=40), :]
+        row = states[pl.ds(place_of(here, r, 5), LAYERS, stride=40), :]
         out[r] = row
         if r >= ROWS - HALO:
             send[r - (ROWS - HALO)] = row
@@ -341,9 +337,10 @@
         send[HALO + j] = row
 
 
-def later_kernel(here, mask, own, far, rate, base, power, power_band, offset_before, *refs):
+def later_kernel(own, far, rate, base, heat, power, power_band, offset_before, *refs):
+    here = position()
     send, jump, *work = refs
-    tile, band = work[:7], work[7:]
+    tile, band = work[:6], work[6:]
     lane = lanes()
     slot = lane & (WIDE - 1)
     left = here[1] == 0
@@ -364,8 +361,8 @@
         band[0][0, i] = row
         band[0][1, i] = row
     advance(
-        tile_part(here, mask, base, power, tile),
-        band_part(here, mask, base, power_band, band),
+        tile_part(base, heat, power, tile),
+        band_part(base, heat, power_band, band),
     )
     for r in range(ROWS):
         f = merged(here, r, band[0], tile[0][0, r])
@@ -413,7 +410,6 @@
 
 def shards(initial_states, coarse_decay, power_map, power_mask, region_ids, region_conductivity):
     slabs = lax.axis_size("tm")
-    here = jnp.stack([lax.axis_index("sx"), lax.axis_index("sy")]).astype(jnp.int32)
     states, powers, decay = (
         x.reshape(LAYERS * ROWS, COLS) for x in (initial_states, power_map, coarse_decay)
     )
@@ -424,19 +420,19 @@
     start, power_own, rate = call(
         load_kernel,
         [plane(ROWS)] * 3,
-        [here],
+        [],
         [pltpu.with_memory_space_constraint(x, pltpu.HBM) for x in (states, powers, decay)],
         "load",
         [VMEM((3, LAYERS * ROWS, COLS), jnp.float32), pltpu.SemaphoreType.DMA((3,))],
         pl.CostEstimate(flops=2_000_000, bytes_accessed=800_000, transcendentals=0),
         pltpu.HBM,
     )
-    sent = call(pack_kernel, plane(2 * SENT + FRINGE), [here], [start, far, power_own, power_far, rate], "pack")
+    sent = call(pack_kernel, plane(2 * SENT + THIN), [], [start, far, power_own, power_far, rate], "pack")
     other = lax.ppermute(sent, "sy", SWAP)
-    end, base, power, band, power_band = call(
+    end, base, heat, power, band, power_band = call(
         tile_kernel,
-        [plane(n) for n in (ROWS, BLOCKS, BOX, PACK, PACK)],
-        [here, mask, region_ids, region_conductivity],
+        [plane(n) for n in (ROWS, BLOCKS, FSTEPS * BLOCKS, BOX, PACK, PACK)],
+        [mask, region_ids, region_conductivity],
         [start, far, power_own, power_far],
         "propagate_tile",
         work_of(BOX),
@@ -445,21 +441,21 @@
     power_band, offset, both = call(
         band_kernel,
         [plane(PACK), plane(ROWS), flat(640)],
-        [here, mask],
-        [end, start, rate, base, band, power_band, other],
+        [],
+        [end, start, rate, base, heat, band, power_band, other],
         "propagate_band",
         [VMEM((PACK, LAYERS, COLS), jnp.float32)] + work_of(PACK),
     )
     both = spread(both, slabs)
     states = spread(call(functools.partial(cycle_kernel, slabs), flat(320), [], [both], "cycle"), slabs)
 
-    own, send = call(turn_kernel, [plane(ROWS + FRINGE), plane(HALO + FRINGE)], [here], [states], "turn")
+    own, send = call(turn_kernel, [plane(ROWS + FRINGE), plane(HALO + FRINGE)], [], [states], "turn")
     far = lax.ppermute(send, "sx", SWAP)
     later, jump = call(
         later_kernel,
         [flat(256), flat(256)],
-        [here, mask],
-        [own, far, rate, base, power, power_band, offset],
+        [],
+        [own, far, rate, base, heat, power, power_band, offset],
         "propagate_later",
         work_of(BOX) + work_of(PACK),
     )

time: 94.1 us -> 90.8 us (0.965)
  Pallas kernels: 14.3 us -> 11.1 us
    pallas_call x8, Pallas kernels: 14.3 us -> 11.1 us  [call(): pl.pallas_call(kernel, out_shape=outs, in_specs=[sspec()] * len(scalars)...]
where the time goes in v4:
time: 90.8 us; the launch traced here: 90.5 us
  blocking collectives  72.7 us (80%)
  Pallas kernels  11.1 us (12%)
  starting transfers between devices  2.84 us (3%)
  waiting for transfers between devices  2.49 us (3%)
    all_to_all x2, blocking collectives, spread(): return lax.all_to_all(x, 'tm', 0, 0, tiled=True).reshape(-1, COLS)  42 us
    all_to_all x1, blocking collectives, shards(): lax.all_to_all(later.reshape(slabs, 4, COLS), 'tm', 0, 0, tiled=True)  15.5 us
    all_to_all x1, blocking collectives, shards(): states = lax.all_to_all(states, 'tm', 0, 0, tiled=True)  15.2 us
    pallas_call x8, Pallas kernels, call(): pl.pallas_call(kernel, out_shape=outs, in_specs=[sspec()] * len(scalars)...  11.1 us
    ppermute x1, starting transfers between devices, shards(): other = lax.ppermute(sent, 'sy', SWAP)  2.16 us
  transfers between devices with their start and end apart: 4, of which 2 were waited for; matrix products, arithmetic and copies ran while one was open for 0% of the time, Pallas kernels for 5%

profile of v4, /device:TPU:16, one launch (start us, length us, event | category | flops | bytes accessed | tf_op | source)
XLA Modules:
  0.0 90.5 jit_solution(9730634491284922161)
XLA Ops:
  0.6 0.1 collective-permute-start
  0.7 0.5 collective-permute-start.1
  1.2 1.3 %load.1 = (f32[32,8,128]{2,1,0:T(8,128)S(1)}, f32[32,8,128]{2,1,0:T(8,128)S(1)}, f32[32,8,128]{2,1,0:T(8,128)S(1)}) custom-call(f32[256,128]{1,0:T(8,128)} %bitcast.21, f32[256,128]{1,0:T(8,128)} %bitcast.23, f32[256,128]{1,0:T(8,128)} %bitcast.19), custom_call_target="tpu_custom_call" | custom-call | flops 2000000 | bytes 800000 | tf_op jit(solution)/shard_map/load/pallas_call | solution.py:51
  2.6 0.0 collective-permute-done.far
  2.6 0.0 collective-permute-done.1.power_far
  2.6 0.0 copy-start
  2.6 0.0 copy-start.1
  2.6 0.2 pack.1
  2.9 0.0 copy-start.2
  2.9 2.2 %collective-permute-start.2 = (f32[22,8,128]{2,1,0:T(8,128)S(1)}, f32[22,8,128]{2,1,0:T(8,128)S(1)}, u32[]{:S(2)}, u32[]{:S(2)}) collective-permute-start(f32[22,8,128]{2,1,0:T(8,128)S(1)} %pack.1), channel_id=1, source_target_pairs={{0,1},{1,0},{2,3},{3,2},{4,5},{5,4},{6,7},{7,6},{8,9},{9,8},{10,11... | collective-permute-start | bytes 270344 | tf_op jit(solution)/shard_map/ppermute | solution.py:431
  5.0 0.0 copy-done
  5.0 0.0 copy-done.1
  5.0 0.0 copy-done.2
  5.0 2.9 %propagate_tile.1 = (f32[32,8,128]{2,1,0:T(8,128)S(1)}, f32[6,8,128]{2,1,0:T(8,128)S(1)}, f32[24,8,128]{2,1,0:T(8,128)S(1)}, f32[44,8,128]{2,1,0:T(8,128)S(1)}, ...) custom-call(s32[4,8]{1,0:T(4,128)S(1)} %bitcast.17, s32[8,8]{1,0:T(8,128)S(1)} %copy-done, f32[4]{0:T(128)S(1)} %copy-done.2, ...), custom_call_target="tpu_custom_call" | custom-call | flops 20000000 | bytes 4000000 | tf_op jit(solution)/shard_map/propagate_tile/pallas_call | solution.py:51
  7.9 1.2 %collective-permute-done.2.other = f32[22,8,128]{2,1,0:T(8,128)S(1)} collective-permute-done((f32[22,8,128]{2,1,0:T(8,128)S(1)}, f32[22,8,128]{2,1,0:T(8,128)S(1)}, u32[]{:S(2)}, u32[]{:S(2)}) %collective-permute-start.2) | collective-permute-done | bytes 90144 | tf_op jit(solution)/shard_map/ppermute | solution.py:431
  9.2 2.1 %propagate_band.1 = (f32[22,8,128]{2,1,0:T(8,128)S(1)}, f32[32,8,128]{2,1,0:T(8,128)S(1)}, f32[640,128]{1,0:T(8,128)S(1)}) custom-call(f32[32,8,128]{2,1,0:T(8,128)S(1)} %get-tuple-element.20.end, f32[32,8,128]{2,1,0:T(8,128)S(1)} %get-tuple-element.18.own.start, f32[32,8,128]{2,1,0:T(8,128)S(1)} %get-tuple-element.21.rate, ...), custom_call_target="tpu_custom_call" | custom-call | tf_op jit(solution)/shard_map/propagate_band/pallas_call | solution.py:51
  11.3 25.5 %all_to_all.20 = f32[64,10,1,128]{3,2,1,0:T(1,128)S(1)} all-to-all(f32[64,10,1,128]{3,2,1,0:T(1,128)S(1)} %bitcast.15), channel_id=1, replica_groups=mesh['tm'=64,'sx'=2,'sy'=2] {'tm'}, dimensions={0} | all-to-all | bytes 655360 | tf_op jit(solution)/shard_map/all_to_all | solution.py:408
  36.8 0.3 cycle.1
  37.0 16.5 %all_to_all.21 = f32[64,5,1,128]{3,2,1,0:T(1,128)S(1)} all-to-all(f32[64,5,1,128]{3,2,1,0:T(1,128)S(1)} %bitcast.14), channel_id=1, replica_groups=mesh['tm'=64,'sx'=2,'sy'=2] {'tm'}, dimensions={0} | all-to-all | bytes 327680 | tf_op jit(solution)/shard_map/all_to_all | solution.py:408
  53.6 0.1 collective-permute-start.3
  53.7 1.3 %collective-permute-done.3.far = f32[20,8,128]{2,1,0:T(8,128)S(1)} collective-permute-done((f32[20,8,128]{2,1,0:T(8,128)S(1)}, f32[20,8,128]{2,1,0:T(8,128)S(1)}, u32[]{:S(2)}, u32[]{:S(2)}) %collective-permute-start.3) | collective-permute-done | bytes 81952 | tf_op jit(solution)/shard_map/ppermute | solution.py:453
  55.0 3.9 %propagate_later.1 = (f32[256,128]{1,0:T(8,128)S(1)}, f32[256,128]{1,0:T(8,128)}) custom-call(f32[40,8,128]{2,1,0:T(8,128)S(1)} %get-tuple-element.27.own, f32[20,8,128]{2,1,0:T(8,128)S(1)} %collective-permute-done.3.far, f32[32,8,128]{2,1,0:T(8,128)S(1)} %get-tuple-element.21.rate, f32[6,8,128]{2,1,0:T(8,128)S(1)} %get-tuple-element.22.base, ...), custom_call_target="tpu_custom_call" | custom-call | tf_op jit(solution)/shard_map/propagate_later/pallas_call | solution.py:51
  58.9 15.5 %all_to_all.22.offset = f32[64,4,128]{2,1,0:T(4,128)S(1)} all-to-all(f32[64,4,128]{2,1,0:T(4,128)S(1)} %bitcast.16), channel_id=1, replica_groups=mesh['tm'=64,'sx'=2,'sy'=2] {'tm'}, dimensions={0} | all-to-all | bytes 262144 | tf_op jit(solution)/shard_map/all_to_all | solution.py:462
  74.4 0.3 cycle_later.1
  74.7 15.2 %all_to_all.23 = f32[64,4,128]{2,1,0:T(4,128)S(1)} all-to-all(f32[64,4,128]{2,1,0:T(4,128)S(1)} %cycle_later.1), channel_id=1, replica_groups=mesh['tm'=64,'sx'=2,'sy'=2] {'tm'}, dimensions={0} | all-to-all | bytes 262144 | tf_op jit(solution)/shard_map/all_to_all | solution.py:467
  89.9 0.7 copy.11
  (1 shorter events, 0.0 us)
Async XLA Ops:
  0.6 2.0 %collective-permute-start = (f32[256,128]{1,0:T(8,128)}, f32[256,128]{1,0:T(8,128)S(1)}, u32[]{:S(2)}, u32[]{:S(2)}) collective-permute-start(f32[256,128]{1,0:T(8,128)} %bitcast.20), channel_id=1, source_target_pairs={{0,2},{2,0},{1,3},{3,1},{4,6},{6,4},{5,7},{7,5},{8,10},{10,8},{9,1... | collective-permute-start | bytes 393224 | tf_op jit(solution)/shard_map/ppermute | solution.py:418
  0.7 1.9 %collective-permute-start.1 = (f32[256,128]{1,0:T(8,128)}, f32[256,128]{1,0:T(8,128)S(1)}, u32[]{:S(2)}, u32[]{:S(2)}) collective-permute-start(f32[256,128]{1,0:T(8,128)} %bitcast.22), channel_id=1, source_target_pairs={{0,2},{2,0},{1,3},{3,1},{4,6},{6,4},{5,7},{7,5},{8,10},{10,8},{9,1... | collective-permute-start | bytes 393224 | tf_op jit(solution)/shard_map/ppermute | solution.py:419
  2.6 2.4 %copy-start = (s32[8,8]{1,0:T(8,128)S(1)}, s32[8,8]{1,0:T(8,128)}, u32[]{:S(2)}) copy-start(s32[8,8]{1,0:T(8,128)} %ids.1) | copy-start | bytes 772
  2.6 2.4 %copy-start.1 = (s32[1,4,8]{2,1,0:T(4,128)S(1)}, s32[1,4,8]{2,1,0:T(4,128)}, u32[]{:S(2)}) copy-start(s32[1,4,8]{2,1,0:T(4,128)} %param.9) | copy-start | bytes 388
  2.9 2.2 %copy-start.2 = (f32[4]{0:T(128)S(1)}, f32[4]{0:T(128)}, u32[]{:S(2)}) copy-start(f32[4]{0:T(128)} %conductivity.1) | copy-start | bytes 52
  2.9 6.3 %collective-permute-start.2 = (f32[22,8,128]{2,1,0:T(8,128)S(1)}, f32[22,8,128]{2,1,0:T(8,128)S(1)}, u32[]{:S(2)}, u32[]{:S(2)}) collective-permute-start(f32[22,8,128]{2,1,0:T(8,128)S(1)} %pack.1), channel_id=1, source_target_pairs={{0,1},{1,0},{2,3},{3,2},{4,5},{5,4},{6,7},{7,6},{8,9},{9,8},{10,11... | collective-permute-start | bytes 270344 | tf_op jit(solution)/shard_map/ppermute | solution.py:431
  53.6 1.4 %collective-permute-start.3 = (f32[20,8,128]{2,1,0:T(8,128)S(1)}, f32[20,8,128]{2,1,0:T(8,128)S(1)}, u32[]{:S(2)}, u32[]{:S(2)}) collective-permute-start(f32[20,8,128]{2,1,0:T(8,128)S(1)} %get-tuple-element.28), channel_id=1, source_target_pairs={{0,2},{2,0},{1,3},{3,1},{4,6},{6,4},{5,7},{7,5},{8,10},{10,8},{9,1... | collective-permute-start | bytes 245768 | tf_op jit(solution)/shard_map/ppermute | solution.py:453

commit v5 on v4

--- a/solution.py
+++ b/solution.py
@@ -88,7 +88,7 @@
 
 
 def place_of(here, r, size):
-    up, down = (x // 4 * size + x % 4 for x in (r, ROWS - 1 - r))
+    up, down = (x // 4 * size + 1 + x % 4 for x in (r, ROWS - 1 - r))
     return jnp.where(here[0] == 0, up, down)
 
 
@@ -130,7 +130,10 @@
             tanh = jnp.tanh(cur)
             cond.append((half * self.base(r)) * (1.0 - cond_slope * tanh))
             source = (half * self.heat(m, r)) * self.power[r] * (1.0 + joule_slope * tanh)
-            self.rhs[r] = (coef_now * cur + coef_old * self.state[old, r]) + source
+            if m:
+                self.rhs[r] = (coef_now * cur + coef_old * self.state[old, r]) + source
+            else:
+                self.rhs[r] = cur + source
         faces = [None] * (n + 1)
         for r in range(1, n):
             faces[r] = cond[r - 1] + cond[r]
@@ -178,24 +181,18 @@
 
 
 def advance(*parts):
-    def turn(t, carry):
-        for now in range(2):
-            old = 1 - now
-            start = (t == 0) if now == 0 else False
-            coef_now = jnp.where(start, 1.0, 4.0 / 3.0).astype(jnp.float32)
-            coef_old = jnp.where(start, 0.0, -1.0 / 3.0).astype(jnp.float32)
-            half = jnp.where(start, 0.5, 1.0 / 3.0).astype(jnp.float32)
-            for part in parts:
-                part.prepare(2 * t + now, now, old, coef_now, coef_old, half)
-            values = [[part.state[now, r] for r in range(part.n)] for part in parts]
-            for k in range(SWEEPS):
-                values = [part.sweep(vs) for part, vs in zip(parts, values)]
-            for part, vs in zip(parts, values):
-                for r in range(part.n):
-                    part.state[old, r] = vs[r]
-        return carry
-
-    lax.fori_loop(0, FSTEPS // 2, turn, 0)
+    for m in range(FSTEPS):
+        now = m % 2
+        old = 1 - now
+        coefs = (4.0 / 3.0, -1.0 / 3.0, 1.0 / 3.0) if m else (1.0, 0.0, 0.5)
+        for part in parts:
+            part.prepare(m, now, old, *coefs)
+        values = [[part.state[now, r] for r in range(part.n)] for part in parts]
+        for k in range(SWEEPS):
+            values = [part.sweep(vs) for part, vs in zip(parts, values)]
+        for part, vs in zip(parts, values):
+            for r in range(part.n):
+                part.state[old, r] = vs[r]
 
 
 def work_of(n):
@@ -305,9 +302,9 @@
         d = rate[r]
         offset = merged(here, r, state, end[r]) - d * start[r]
         offset_out[r] = offset
-        at = place_of(here, r, 10)
-        send[pl.ds(at, LAYERS, stride=80), :] = d
-        send[pl.ds(at + 5, LAYERS, stride=80), :] = offset
+        at = place_of(here, r, 9)
+        send[pl.ds(at, LAYERS, stride=72), :] = d
+        send[pl.ds(at + 4, LAYERS, stride=72), :] = offset
     back = COLS - fringe_shift(left)
     for j in range(FRINGE):
         first, last = None, None
@@ -319,9 +316,7 @@
             first = u if g == 0 else jnp.where(lane < g * 32, first, u)
             last = f if g == 0 else jnp.where(lane < g * 32, last, f)
         d = moved(other[2 * SENT + j % THIN], -16 * (j // THIN))
-        d = jnp.where((lane & 31) < HALO, d, 0.0)
-        send[pl.ds(j * 80 + 4, LAYERS, stride=10), :] = d
-        send[pl.ds(j * 80 + 9, LAYERS, stride=10), :] = last - d * first
+        send[pl.ds(j * 72, LAYERS, stride=9), :] = jnp.where((lane & 31) < 16, d, moved(last - d * first, 16))
 
 
 def turn_kernel(states, out, send):
@@ -332,7 +327,7 @@
         if r >= ROWS - HALO:
             send[r - (ROWS - HALO)] = row
     for j in range(FRINGE):
-        row = states[pl.ds(j * 40 + 4, LAYERS, stride=5), :]
+        row = states[pl.ds(j * 40, LAYERS, stride=5), :]
         out[ROWS + j] = row
         send[HALO + j] = row
 
@@ -390,14 +385,24 @@
     def store(k, u):
         out[5 * k:5 * k + 5] = u
 
-    solve(slabs, lambda k: both[10 * k:10 * k + 5], lambda k: both[10 * k + 5:10 * k + 10], store)
+    row = lax.broadcasted_iota(jnp.int32, (5, COLS), 0)
+    slot = lax.broadcasted_iota(jnp.int32, (5, COLS), 1) & 31
+    empty = (row == 0) & (slot >= HALO)
+
+    def rate(k):
+        return jnp.where(empty, 0.0, both[9 * k:9 * k + 5])
+
+    def offset(k):
+        return jnp.where(row == 0, moved(both[9 * k:9 * k + 5], -16), both[9 * k + 4:9 * k + 9])
+
+    solve(slabs, rate, offset, store)
 
 
 def cycle_later_kernel(slabs, both, offset, out):
     def store(k, u):
         out[k] = u
 
-    solve(slabs, lambda k: both[10 * k:10 * k + 4], lambda k: offset[k], store)
+    solve(slabs, lambda k: both[9 * k + 1:9 * k + 5], lambda k: offset[k], store)
 
 
 SWAP = [(0, 1), (1, 0)]
@@ -440,7 +445,7 @@
     )
     power_band, offset, both = call(
         band_kernel,
-        [plane(PACK), plane(ROWS), flat(640)],
+        [plane(PACK), plane(ROWS), flat(576)],
         [],
         [end, start, rate, base, heat, band, power_band, other],
         "propagate_band",

time: 90.8 us -> 89.8 us (0.989)
  transfers between devices with their start and end apart: 4 -> 4, of which waited for: 2 -> 2; matrix products, arithmetic and copies ran while one was open for 0% -> 0% of each run, Pallas kernels for 5% -> 4%
where the time goes in v5:
time: 89.8 us; the launch traced here: 89.5 us
  blocking collectives  72 us (80%)
  Pallas kernels  10.4 us (12%)
  waiting for transfers between devices  2.87 us (3%)
  starting transfers between devices  2.84 us (3%)
    all_to_all x2, blocking collectives, spread(): return lax.all_to_all(x, 'tm', 0, 0, tiled=True).reshape(-1, COLS)  41.3 us
    all_to_all x1, blocking collectives, shards(): lax.all_to_all(later.reshape(slabs, 4, COLS), 'tm', 0, 0, tiled=True)  15.5 us
    all_to_all x1, blocking collectives, shards(): states = lax.all_to_all(states, 'tm', 0, 0, tiled=True)  15.2 us
    pallas_call x8, Pallas kernels, call(): pl.pallas_call(kernel, out_shape=outs, in_specs=[sspec()] * len(scalars)...  10.4 us
    ppermute x1, starting transfers between devices, shards(): other = lax.ppermute(sent, 'sy', SWAP)  2.16 us
  transfers between devices with their start and end apart: 4, of which 2 were waited for; matrix products, arithmetic and copies ran while one was open for 0% of the time, Pallas kernels for 4%

profile of v5, /device:TPU:16, one launch (start us, length us, event | category | flops | bytes accessed | tf_op | source)
XLA Modules:
  0.0 89.5 jit_solution(17374993643190189457)
XLA Ops:
  0.6 0.1 collective-permute-start
  0.7 0.5 collective-permute-start.1
  1.2 1.3 %load.1 = (f32[32,8,128]{2,1,0:T(8,128)S(1)}, f32[32,8,128]{2,1,0:T(8,128)S(1)}, f32[32,8,128]{2,1,0:T(8,128)S(1)}) custom-call(f32[256,128]{1,0:T(8,128)} %bitcast.21, f32[256,128]{1,0:T(8,128)} %bitcast.23, f32[256,128]{1,0:T(8,128)} %bitcast.19), custom_call_target="tpu_custom_call" | custom-call | flops 2000000 | bytes 800000 | tf_op jit(solution)/shard_map/load/pallas_call | solution.py:51
  2.6 0.0 collective-permute-done.far
  2.6 0.0 collective-permute-done.1.power_far
  2.6 0.0 copy-start
  2.6 0.0 copy-start.1
  2.6 0.2 pack.1
  2.9 0.0 copy-start.2
  2.9 2.2 %collective-permute-start.2 = (f32[22,8,128]{2,1,0:T(8,128)S(1)}, f32[22,8,128]{2,1,0:T(8,128)S(1)}, u32[]{:S(2)}, u32[]{:S(2)}) collective-permute-start(f32[22,8,128]{2,1,0:T(8,128)S(1)} %pack.1), channel_id=1, source_target_pairs={{0,1},{1,0},{2,3},{3,2},{4,5},{5,4},{6,7},{7,6},{8,9},{9,8},{10,11... | collective-permute-start | bytes 270344 | tf_op jit(solution)/shard_map/ppermute | solution.py:436
  5.0 0.0 copy-done
  5.0 0.0 copy-done.1
  5.0 0.0 copy-done.2
  5.0 2.5 %propagate_tile.1 = (f32[32,8,128]{2,1,0:T(8,128)S(1)}, f32[6,8,128]{2,1,0:T(8,128)S(1)}, f32[24,8,128]{2,1,0:T(8,128)S(1)}, f32[44,8,128]{2,1,0:T(8,128)S(1)}, ...) custom-call(s32[4,8]{1,0:T(4,128)S(1)} %bitcast.17, s32[8,8]{1,0:T(8,128)S(1)} %copy-done, f32[4]{0:T(128)S(1)} %copy-done.2, ...), custom_call_target="tpu_custom_call" | custom-call | flops 20000000 | bytes 4000000 | tf_op jit(solution)/shard_map/propagate_tile/pallas_call | solution.py:51
  7.5 1.6 %collective-permute-done.2.other = f32[22,8,128]{2,1,0:T(8,128)S(1)} collective-permute-done((f32[22,8,128]{2,1,0:T(8,128)S(1)}, f32[22,8,128]{2,1,0:T(8,128)S(1)}, u32[]{:S(2)}, u32[]{:S(2)}) %collective-permute-start.2) | collective-permute-done | bytes 90144 | tf_op jit(solution)/shard_map/ppermute | solution.py:436
  9.2 2.1 %propagate_band.1 = (f32[22,8,128]{2,1,0:T(8,128)S(1)}, f32[32,8,128]{2,1,0:T(8,128)S(1)}, f32[576,128]{1,0:T(8,128)S(1)}) custom-call(f32[32,8,128]{2,1,0:T(8,128)S(1)} %get-tuple-element.20.end, f32[32,8,128]{2,1,0:T(8,128)S(1)} %get-tuple-element.18.own.start, f32[32,8,128]{2,1,0:T(8,128)S(1)} %get-tuple-element.21.rate, ...), custom_call_target="tpu_custom_call" | custom-call | tf_op jit(solution)/shard_map/propagate_band/pallas_call | solution.py:51
  11.3 24.7 %all_to_all.20 = f32[64,9,1,128]{3,2,1,0:T(1,128)S(1)} all-to-all(f32[64,9,1,128]{3,2,1,0:T(1,128)S(1)} %bitcast.15), channel_id=1, replica_groups=mesh['tm'=64,'sx'=2,'sy'=2] {'tm'}, dimensions={0} | all-to-all | bytes 589824 | tf_op jit(solution)/shard_map/all_to_all | solution.py:413
  36.0 0.3 cycle.1
  36.4 16.6 %all_to_all.21 = f32[64,5,1,128]{3,2,1,0:T(1,128)S(1)} all-to-all(f32[64,5,1,128]{3,2,1,0:T(1,128)S(1)} %bitcast.13), channel_id=1, replica_groups=mesh['tm'=64,'sx'=2,'sy'=2] {'tm'}, dimensions={0} | all-to-all | bytes 327680 | tf_op jit(solution)/shard_map/all_to_all | solution.py:413
  53.0 0.1 collective-permute-start.3
  53.1 1.3 %collective-permute-done.3.far = f32[20,8,128]{2,1,0:T(8,128)S(1)} collective-permute-done((f32[20,8,128]{2,1,0:T(8,128)S(1)}, f32[20,8,128]{2,1,0:T(8,128)S(1)}, u32[]{:S(2)}, u32[]{:S(2)}) %collective-permute-start.3) | collective-permute-done | bytes 81952 | tf_op jit(solution)/shard_map/ppermute | solution.py:458
  54.3 3.6 %propagate_later.1 = (f32[256,128]{1,0:T(8,128)S(1)}, f32[256,128]{1,0:T(8,128)}) custom-call(f32[40,8,128]{2,1,0:T(8,128)S(1)} %get-tuple-element.27.own, f32[20,8,128]{2,1,0:T(8,128)S(1)} %collective-permute-done.3.far, f32[32,8,128]{2,1,0:T(8,128)S(1)} %get-tuple-element.21.rate, f32[6,8,128]{2,1,0:T(8,128)S(1)} %get-tuple-element.22.base, ...), custom_call_target="tpu_custom_call" | custom-call | tf_op jit(solution)/shard_map/propagate_later/pallas_call | solution.py:51
  57.9 15.5 %all_to_all.22.offset = f32[64,4,128]{2,1,0:T(4,128)S(1)} all-to-all(f32[64,4,128]{2,1,0:T(4,128)S(1)} %bitcast.16), channel_id=1, replica_groups=mesh['tm'=64,'sx'=2,'sy'=2] {'tm'}, dimensions={0} | all-to-all | bytes 262144 | tf_op jit(solution)/shard_map/all_to_all | solution.py:467
  73.4 0.3 cycle_later.1
  73.6 15.2 %all_to_all.23 = f32[64,4,128]{2,1,0:T(4,128)S(1)} all-to-all(f32[64,4,128]{2,1,0:T(4,128)S(1)} %cycle_later.1), channel_id=1, replica_groups=mesh['tm'=64,'sx'=2,'sy'=2] {'tm'}, dimensions={0} | all-to-all | bytes 262144 | tf_op jit(solution)/shard_map/all_to_all | solution.py:472
  88.8 0.7 copy.11
  (1 shorter events, 0.0 us)
Async XLA Ops:
  0.6 2.0 %collective-permute-start = (f32[256,128]{1,0:T(8,128)}, f32[256,128]{1,0:T(8,128)S(1)}, u32[]{:S(2)}, u32[]{:S(2)}) collective-permute-start(f32[256,128]{1,0:T(8,128)} %bitcast.20), channel_id=1, source_target_pairs={{0,2},{2,0},{1,3},{3,1},{4,6},{6,4},{5,7},{7,5},{8,10},{10,8},{9,1... | collective-permute-start | bytes 393224 | tf_op jit(solution)/shard_map/ppermute | solution.py:423
  0.7 1.9 %collective-permute-start.1 = (f32[256,128]{1,0:T(8,128)}, f32[256,128]{1,0:T(8,128)S(1)}, u32[]{:S(2)}, u32[]{:S(2)}) collective-permute-start(f32[256,128]{1,0:T(8,128)} %bitcast.22), channel_id=1, source_target_pairs={{0,2},{2,0},{1,3},{3,1},{4,6},{6,4},{5,7},{7,5},{8,10},{10,8},{9,1... | collective-permute-start | bytes 393224 | tf_op jit(solution)/shard_map/ppermute | solution.py:424
  2.6 2.4 %copy-start = (s32[8,8]{1,0:T(8,128)S(1)}, s32[8,8]{1,0:T(8,128)}, u32[]{:S(2)}) copy-start(s32[8,8]{1,0:T(8,128)} %ids.1) | copy-start | bytes 772
  2.6 2.4 %copy-start.1 = (s32[1,4,8]{2,1,0:T(4,128)S(1)}, s32[1,4,8]{2,1,0:T(4,128)}, u32[]{:S(2)}) copy-start(s32[1,4,8]{2,1,0:T(4,128)} %param.9) | copy-start | bytes 388
  2.9 2.2 %copy-start.2 = (f32[4]{0:T(128)S(1)}, f32[4]{0:T(128)}, u32[]{:S(2)}) copy-start(f32[4]{0:T(128)} %conductivity.1) | copy-start | bytes 52
  2.9 6.3 %collective-permute-start.2 = (f32[22,8,128]{2,1,0:T(8,128)S(1)}, f32[22,8,128]{2,1,0:T(8,128)S(1)}, u32[]{:S(2)}, u32[]{:S(2)}) collective-permute-start(f32[22,8,128]{2,1,0:T(8,128)S(1)} %pack.1), channel_id=1, source_target_pairs={{0,1},{1,0},{2,3},{3,2},{4,5},{5,4},{6,7},{7,6},{8,9},{9,8},{10,11... | collective-permute-start | bytes 270344 | tf_op jit(solution)/shard_map/ppermute | solution.py:436
  53.0 1.4 %collective-permute-start.3 = (f32[20,8,128]{2,1,0:T(8,128)S(1)}, f32[20,8,128]{2,1,0:T(8,128)S(1)}, u32[]{:S(2)}, u32[]{:S(2)}) collective-permute-start(f32[20,8,128]{2,1,0:T(8,128)S(1)} %get-tuple-element.28), channel_id=1, source_target_pairs={{0,2},{2,0},{1,3},{3,1},{4,6},{6,4},{5,7},{7,5},{8,10},{10,8},{9,1... | collective-permute-start | bytes 245768 | tf_op jit(solution)/shard_map/ppermute | solution.py:458

commit v6 on v5

--- a/solution.py
+++ b/solution.py
@@ -398,11 +398,15 @@
     solve(slabs, rate, offset, store)
 
 
-def cycle_later_kernel(slabs, both, offset, out):
+def cycle_later_kernel(slabs, both, offset, jump, out, jump_out, sem):
+    copy = pltpu.make_async_copy(jump, jump_out, sem)
+    copy.start()
+
     def store(k, u):
         out[k] = u
 
     solve(slabs, lambda k: both[9 * k + 1:9 * k + 5], lambda k: offset[k], store)
+    copy.wait()
 
 
 SWAP = [(0, 1), (1, 0)]
@@ -465,10 +469,15 @@
         work_of(BOX) + work_of(PACK),
     )
     later = lax.all_to_all(later.reshape(slabs, 4, COLS), "tm", 0, 0, tiled=True)
-    states = call(
+    states, jump = pl.pallas_call(
         functools.partial(cycle_later_kernel, slabs),
-        jax.ShapeDtypeStruct((slabs, 4, COLS), jnp.float32), [], [both, later], "cycle_later",
-    )
+        out_shape=[jax.ShapeDtypeStruct((slabs, 4, COLS), jnp.float32), flat(LAYERS * ROWS)],
+        in_specs=[spec()] * 3,
+        out_specs=[spec(), pl.BlockSpec(memory_space=pl.ANY)],
+        scratch_shapes=[pltpu.SemaphoreType.DMA],
+        compiler_params=pltpu.CompilerParams(vmem_limit_bytes=8 * 1024 * 1024),
+        name="cycle_later",
+    )(both, later, jump)
     states = lax.all_to_all(states, "tm", 0, 0, tiled=True)
     shape = (1, LAYERS, ROWS, COLS)
     return states.reshape(shape), jump.reshape(shape)

time: 89.8 us -> 89.5 us (level)
    pallas_call x8 -> x7, Pallas kernels: 10.4 us -> 9.52 us  [call(): pl.pallas_call(kernel, out_shape=outs, in_specs=[sspec()] * len(scalars)...]
where the time goes in v6:
time: 89.5 us; the launch traced here: 89.3 us
  blocking collectives  72 us (80%)
  Pallas kernels  10.2 us (11%)
  waiting for transfers between devices  2.85 us (3%)
  starting transfers between devices  2.84 us (3%)
    all_to_all x2, blocking collectives, spread(): return lax.all_to_all(x, 'tm', 0, 0, tiled=True).reshape(-1, COLS)  41.3 us
    all_to_all x1, blocking collectives, shards(): lax.all_to_all(later.reshape(slabs, 4, COLS), 'tm', 0, 0, tiled=True)  15.5 us
    all_to_all x1, blocking collectives, shards(): states = lax.all_to_all(states, 'tm', 0, 0, tiled=True)  15.2 us
    pallas_call x7, Pallas kernels, call(): pl.pallas_call(kernel, out_shape=outs, in_specs=[sspec()] * len(scalars)...  9.52 us
    ppermute x1, starting transfers between devices, shards(): other = lax.ppermute(sent, 'sy', SWAP)  2.16 us
  transfers between devices with their start and end apart: 4, of which 2 were waited for; matrix products, arithmetic and copies ran while one was open for 0% of the time, Pallas kernels for 4%

profile of v6, /device:TPU:16, one launch (start us, length us, event | category | flops | bytes accessed | tf_op | source)
XLA Modules:
  0.0 89.3 jit_solution(4027214546630367419)
XLA Ops:
  0.6 0.1 collective-permute-start
  0.7 0.5 collective-permute-start.1
  1.2 1.3 %load.1 = (f32[32,8,128]{2,1,0:T(8,128)S(1)}, f32[32,8,128]{2,1,0:T(8,128)S(1)}, f32[32,8,128]{2,1,0:T(8,128)S(1)}) custom-call(f32[256,128]{1,0:T(8,128)} %bitcast.21, f32[256,128]{1,0:T(8,128)} %bitcast.23, f32[256,128]{1,0:T(8,128)} %bitcast.19), custom_call_target="tpu_custom_call" | custom-call | flops 2000000 | bytes 800000 | tf_op jit(solution)/shard_map/load/pallas_call | solution.py:51
  2.6 0.0 collective-permute-done.far
  2.6 0.0 collective-permute-done.1.power_far
  2.6 0.0 copy-start
  2.6 0.0 copy-start.1
  2.6 0.2 pack.1
  2.9 0.0 copy-start.2
  2.9 2.2 %collective-permute-start.2 = (f32[22,8,128]{2,1,0:T(8,128)S(1)}, f32[22,8,128]{2,1,0:T(8,128)S(1)}, u32[]{:S(2)}, u32[]{:S(2)}) collective-permute-start(f32[22,8,128]{2,1,0:T(8,128)S(1)} %pack.1), channel_id=1, source_target_pairs={{0,1},{1,0},{2,3},{3,2},{4,5},{5,4},{6,7},{7,6},{8,9},{9,8},{10,11... | collective-permute-start | bytes 270344 | tf_op jit(solution)/shard_map/ppermute | solution.py:440
  5.0 0.0 copy-done
  5.0 0.0 copy-done.1
  5.0 0.0 copy-done.2
  5.0 2.5 %propagate_tile.1 = (f32[32,8,128]{2,1,0:T(8,128)S(1)}, f32[6,8,128]{2,1,0:T(8,128)S(1)}, f32[24,8,128]{2,1,0:T(8,128)S(1)}, f32[44,8,128]{2,1,0:T(8,128)S(1)}, ...) custom-call(s32[4,8]{1,0:T(4,128)S(1)} %bitcast.17, s32[8,8]{1,0:T(8,128)S(1)} %copy-done, f32[4]{0:T(128)S(1)} %copy-done.2, ...), custom_call_target="tpu_custom_call" | custom-call | flops 20000000 | bytes 4000000 | tf_op jit(solution)/shard_map/propagate_tile/pallas_call | solution.py:51
  7.6 1.6 %collective-permute-done.2.other = f32[22,8,128]{2,1,0:T(8,128)S(1)} collective-permute-done((f32[22,8,128]{2,1,0:T(8,128)S(1)}, f32[22,8,128]{2,1,0:T(8,128)S(1)}, u32[]{:S(2)}, u32[]{:S(2)}) %collective-permute-start.2) | collective-permute-done | bytes 90144 | tf_op jit(solution)/shard_map/ppermute | solution.py:440
  9.2 2.1 %propagate_band.1 = (f32[22,8,128]{2,1,0:T(8,128)S(1)}, f32[32,8,128]{2,1,0:T(8,128)S(1)}, f32[576,128]{1,0:T(8,128)S(1)}) custom-call(f32[32,8,128]{2,1,0:T(8,128)S(1)} %get-tuple-element.22.end, f32[32,8,128]{2,1,0:T(8,128)S(1)} %get-tuple-element.20.own.start, f32[32,8,128]{2,1,0:T(8,128)S(1)} %get-tuple-element.23.rate, ...), custom_call_target="tpu_custom_call" | custom-call | tf_op jit(solution)/shard_map/propagate_band/pallas_call | solution.py:51
  11.3 24.7 %all_to_all.20 = f32[64,9,1,128]{3,2,1,0:T(1,128)S(1)} all-to-all(f32[64,9,1,128]{3,2,1,0:T(1,128)S(1)} %bitcast.15), channel_id=1, replica_groups=mesh['tm'=64,'sx'=2,'sy'=2] {'tm'}, dimensions={0} | all-to-all | bytes 589824 | tf_op jit(solution)/shard_map/all_to_all | solution.py:417
  36.0 0.3 cycle.1
  36.3 16.6 %all_to_all.21 = f32[64,5,1,128]{3,2,1,0:T(1,128)S(1)} all-to-all(f32[64,5,1,128]{3,2,1,0:T(1,128)S(1)} %bitcast.13), channel_id=1, replica_groups=mesh['tm'=64,'sx'=2,'sy'=2] {'tm'}, dimensions={0} | all-to-all | bytes 327680 | tf_op jit(solution)/shard_map/all_to_all | solution.py:417
  53.0 0.1 collective-permute-start.3
  53.1 1.3 %collective-permute-done.3.far = f32[20,8,128]{2,1,0:T(8,128)S(1)} collective-permute-done((f32[20,8,128]{2,1,0:T(8,128)S(1)}, f32[20,8,128]{2,1,0:T(8,128)S(1)}, u32[]{:S(2)}, u32[]{:S(2)}) %collective-permute-start.3) | collective-permute-done | bytes 81952 | tf_op jit(solution)/shard_map/ppermute | solution.py:462
  54.3 2.9 %propagate_later.1 = (f32[256,128]{1,0:T(8,128)S(1)}, f32[256,128]{1,0:T(8,128)S(1)}) custom-call(f32[40,8,128]{2,1,0:T(8,128)S(1)} %get-tuple-element.29.own, f32[20,8,128]{2,1,0:T(8,128)S(1)} %collective-permute-done.3.far, f32[32,8,128]{2,1,0:T(8,128)S(1)} %get-tuple-element.23.rate, f32[6,8,128]{2,1,0:T(8,128)S(1)} %get-tuple-element.24.base, ...), custom_call_target="tpu_custom_call" | custom-call | tf_op jit(solution)/shard_map/propagate_later/pallas_call | solution.py:51
  57.3 15.5 %all_to_all.22.offset = f32[64,4,128]{2,1,0:T(4,128)S(1)} all-to-all(f32[64,4,128]{2,1,0:T(4,128)S(1)} %bitcast.16), channel_id=1, replica_groups=mesh['tm'=64,'sx'=2,'sy'=2] {'tm'}, dimensions={0} | all-to-all | bytes 262144 | tf_op jit(solution)/shard_map/all_to_all | solution.py:471
  72.7 0.7 cycle_later.1
  73.4 15.2 %all_to_all.23 = f32[64,4,128]{2,1,0:T(4,128)S(1)} all-to-all(f32[64,4,128]{2,1,0:T(4,128)S(1)} %get-tuple-element.36), channel_id=1, replica_groups=mesh['tm'=64,'sx'=2,'sy'=2] {'tm'}, dimensions={0} | all-to-all | bytes 262144 | tf_op jit(solution)/shard_map/all_to_all | solution.py:481
  88.6 0.7 copy.11
  (1 shorter events, 0.0 us)
Async XLA Ops:
  0.6 2.0 %collective-permute-start = (f32[256,128]{1,0:T(8,128)}, f32[256,128]{1,0:T(8,128)S(1)}, u32[]{:S(2)}, u32[]{:S(2)}) collective-permute-start(f32[256,128]{1,0:T(8,128)} %bitcast.20), channel_id=1, source_target_pairs={{0,2},{2,0},{1,3},{3,1},{4,6},{6,4},{5,7},{7,5},{8,10},{10,8},{9,1... | collective-permute-start | bytes 393224 | tf_op jit(solution)/shard_map/ppermute | solution.py:427
  0.7 1.9 %collective-permute-start.1 = (f32[256,128]{1,0:T(8,128)}, f32[256,128]{1,0:T(8,128)S(1)}, u32[]{:S(2)}, u32[]{:S(2)}) collective-permute-start(f32[256,128]{1,0:T(8,128)} %bitcast.22), channel_id=1, source_target_pairs={{0,2},{2,0},{1,3},{3,1},{4,6},{6,4},{5,7},{7,5},{8,10},{10,8},{9,1... | collective-permute-start | bytes 393224 | tf_op jit(solution)/shard_map/ppermute | solution.py:428
  2.6 2.4 %copy-start = (s32[8,8]{1,0:T(8,128)S(1)}, s32[8,8]{1,0:T(8,128)}, u32[]{:S(2)}) copy-start(s32[8,8]{1,0:T(8,128)} %ids.1) | copy-start | bytes 772
  2.6 2.4 %copy-start.1 = (s32[1,4,8]{2,1,0:T(4,128)S(1)}, s32[1,4,8]{2,1,0:T(4,128)}, u32[]{:S(2)}) copy-start(s32[1,4,8]{2,1,0:T(4,128)} %param.9) | copy-start | bytes 388
  2.9 2.2 %copy-start.2 = (f32[4]{0:T(128)S(1)}, f32[4]{0:T(128)}, u32[]{:S(2)}) copy-start(f32[4]{0:T(128)} %conductivity.1) | copy-start | bytes 52
  2.9 6.3 %collective-permute-start.2 = (f32[22,8,128]{2,1,0:T(8,128)S(1)}, f32[22,8,128]{2,1,0:T(8,128)S(1)}, u32[]{:S(2)}, u32[]{:S(2)}) collective-permute-start(f32[22,8,128]{2,1,0:T(8,128)S(1)} %pack.1), channel_id=1, source_target_pairs={{0,1},{1,0},{2,3},{3,2},{4,5},{5,4},{6,7},{7,6},{8,9},{9,8},{10,11... | collective-permute-start | bytes 270344 | tf_op jit(solution)/shard_map/ppermute | solution.py:440
  53.0 1.4 %collective-permute-start.3 = (f32[20,8,128]{2,1,0:T(8,128)S(1)}, f32[20,8,128]{2,1,0:T(8,128)S(1)}, u32[]{:S(2)}, u32[]{:S(2)}) collective-permute-start(f32[20,8,128]{2,1,0:T(8,128)S(1)} %get-tuple-element.30), channel_id=1, source_target_pairs={{0,2},{2,0},{1,3},{3,1},{4,6},{6,4},{5,7},{7,5},{8,10},{10,8},{9,1... | collective-permute-start | bytes 245768 | tf_op jit(solution)/shard_map/ppermute | solution.py:462

commit v7 on v6

--- a/solution.py
+++ b/solution.py
@@ -254,7 +254,6 @@
     for r in range(BOX):
         row = box_row(here, own, far, r)
         state[0, r] = row
-        state[1, r] = row
         power[r] = box_row(here, power_own, power_far, r)
     for i in range(PACK):
         band[i] = banded(i, lambda r: state[0, r])
@@ -294,7 +293,6 @@
     for i in range(PACK):
         row = jnp.where(mine, band[i], received(0, i))
         state[0, i] = row
-        state[1, i] = row
         first_band[i] = row
         power[i] = jnp.where(mine, power_own[i], received(1, i))
     advance(band_part(base, heat, power, work))
@@ -344,7 +342,6 @@
     for r in range(BOX):
         row = own[r] if r < ROWS else far[BOX - 1 - r]
         tile[0][0, r] = row
-        tile[0][1, r] = row
     for i in range(PACK):
         parts = []
         for g in range(2):
@@ -354,7 +351,6 @@
         beside = jnp.where(lane < WIDE, parts[0], parts[1])
         row = jnp.where(fringe, beside, banded(i, lambda r: tile[0][0, r]))
         band[0][0, i] = row
-        band[0][1, i] = row
     advance(
         tile_part(base, heat, power, tile),
         band_part(base, heat, power_band, band),

time: 89.5 us -> 89.5 us (level)
  no operation moved by 1% of the time
where the time goes in v7:
time: 89.5 us; the launch traced here: 89.3 us
  blocking collectives  72 us (80%)
  Pallas kernels  10.2 us (11%)
  waiting for transfers between devices  2.85 us (3%)
  starting transfers between devices  2.84 us (3%)
    all_to_all x2, blocking collectives, spread(): return lax.all_to_all(x, 'tm', 0, 0, tiled=True).reshape(-1, COLS)  41.3 us
    all_to_all x1, blocking collectives, shards(): lax.all_to_all(later.reshape(slabs, 4, COLS), 'tm', 0, 0, tiled=True)  15.5 us
    all_to_all x1, blocking collectives, shards(): states = lax.all_to_all(states, 'tm', 0, 0, tiled=True)  15.2 us
    pallas_call x7, Pallas kernels, call(): pl.pallas_call(kernel, out_shape=outs, in_specs=[sspec()] * len(scalars)...  9.52 us
    ppermute x1, starting transfers between devices, shards(): other = lax.ppermute(sent, 'sy', SWAP)  2.16 us
  transfers between devices with their start and end apart: 4, of which 2 were waited for; matrix products, arithmetic and copies ran while one was open for 0% of the time, Pallas kernels for 4%

profile of v7, /device:TPU:16, one launch (start us, length us, event | category | flops | bytes accessed | tf_op | source)
XLA Modules:
  0.0 89.3 jit_solution(4027214546630367419)
XLA Ops:
  0.6 0.1 collective-permute-start
  0.7 0.5 collective-permute-start.1
  1.2 1.3 %load.1 = (f32[32,8,128]{2,1,0:T(8,128)S(1)}, f32[32,8,128]{2,1,0:T(8,128)S(1)}, f32[32,8,128]{2,1,0:T(8,128)S(1)}) custom-call(f32[256,128]{1,0:T(8,128)} %bitcast.21, f32[256,128]{1,0:T(8,128)} %bitcast.23, f32[256,128]{1,0:T(8,128)} %bitcast.19), custom_call_target="tpu_custom_call" | custom-call | flops 2000000 | bytes 800000 | tf_op jit(solution)/shard_map/load/pallas_call | solution.py:51
  2.6 0.0 collective-permute-done.far
  2.6 0.0 collective-permute-done.1.power_far
  2.6 0.0 copy-start
  2.6 0.0 copy-start.1
  2.6 0.2 pack.1
  2.9 0.0 copy-start.2
  2.9 2.2 %collective-permute-start.2 = (f32[22,8,128]{2,1,0:T(8,128)S(1)}, f32[22,8,128]{2,1,0:T(8,128)S(1)}, u32[]{:S(2)}, u32[]{:S(2)}) collective-permute-start(f32[22,8,128]{2,1,0:T(8,128)S(1)} %pack.1), channel_id=1, source_target_pairs={{0,1},{1,0},{2,3},{3,2},{4,5},{5,4},{6,7},{7,6},{8,9},{9,8},{10,11... | collective-permute-start | bytes 270344 | tf_op jit(solution)/shard_map/ppermute | solution.py:436
  5.0 0.0 copy-done
  5.0 0.0 copy-done.1
  5.0 0.0 copy-done.2
  5.0 2.5 %propagate_tile.1 = (f32[32,8,128]{2,1,0:T(8,128)S(1)}, f32[6,8,128]{2,1,0:T(8,128)S(1)}, f32[24,8,128]{2,1,0:T(8,128)S(1)}, f32[44,8,128]{2,1,0:T(8,128)S(1)}, ...) custom-call(s32[4,8]{1,0:T(4,128)S(1)} %bitcast.17, s32[8,8]{1,0:T(8,128)S(1)} %copy-done, f32[4]{0:T(128)S(1)} %copy-done.2, ...), custom_call_target="tpu_custom_call" | custom-call | flops 20000000 | bytes 4000000 | tf_op jit(solution)/shard_map/propagate_tile/pallas_call | solution.py:51
  7.6 1.6 %collective-permute-done.2.other = f32[22,8,128]{2,1,0:T(8,128)S(1)} collective-permute-done((f32[22,8,128]{2,1,0:T(8,128)S(1)}, f32[22,8,128]{2,1,0:T(8,128)S(1)}, u32[]{:S(2)}, u32[]{:S(2)}) %collective-permute-start.2) | collective-permute-done | bytes 90144 | tf_op jit(solution)/shard_map/ppermute | solution.py:436
  9.2 2.1 %propagate_band.1 = (f32[22,8,128]{2,1,0:T(8,128)S(1)}, f32[32,8,128]{2,1,0:T(8,128)S(1)}, f32[576,128]{1,0:T(8,128)S(1)}) custom-call(f32[32,8,128]{2,1,0:T(8,128)S(1)} %get-tuple-element.22.end, f32[32,8,128]{2,1,0:T(8,128)S(1)} %get-tuple-element.20.own.start, f32[32,8,128]{2,1,0:T(8,128)S(1)} %get-tuple-element.23.rate, ...), custom_call_target="tpu_custom_call" | custom-call | tf_op jit(solution)/shard_map/propagate_band/pallas_call | solution.py:51
  11.3 24.7 %all_to_all.20 = f32[64,9,1,128]{3,2,1,0:T(1,128)S(1)} all-to-all(f32[64,9,1,128]{3,2,1,0:T(1,128)S(1)} %bitcast.15), channel_id=1, replica_groups=mesh['tm'=64,'sx'=2,'sy'=2] {'tm'}, dimensions={0} | all-to-all | bytes 589824 | tf_op jit(solution)/shard_map/all_to_all | solution.py:413
  36.0 0.3 cycle.1
  36.3 16.6 %all_to_all.21 = f32[64,5,1,128]{3,2,1,0:T(1,128)S(1)} all-to-all(f32[64,5,1,128]{3,2,1,0:T(1,128)S(1)} %bitcast.13), channel_id=1, replica_groups=mesh['tm'=64,'sx'=2,'sy'=2] {'tm'}, dimensions={0} | all-to-all | bytes 327680 | tf_op jit(solution)/shard_map/all_to_all | solution.py:413
  53.0 0.1 collective-permute-start.3
  53.1 1.3 %collective-permute-done.3.far = f32[20,8,128]{2,1,0:T(8,128)S(1)} collective-permute-done((f32[20,8,128]{2,1,0:T(8,128)S(1)}, f32[20,8,128]{2,1,0:T(8,128)S(1)}, u32[]{:S(2)}, u32[]{:S(2)}) %collective-permute-start.3) | collective-permute-done | bytes 81952 | tf_op jit(solution)/shard_map/ppermute | solution.py:458
  54.3 2.9 %propagate_later.1 = (f32[256,128]{1,0:T(8,128)S(1)}, f32[256,128]{1,0:T(8,128)S(1)}) custom-call(f32[40,8,128]{2,1,0:T(8,128)S(1)} %get-tuple-element.29.own, f32[20,8,128]{2,1,0:T(8,128)S(1)} %collective-permute-done.3.far, f32[32,8,128]{2,1,0:T(8,128)S(1)} %get-tuple-element.23.rate, f32[6,8,128]{2,1,0:T(8,128)S(1)} %get-tuple-element.24.base, ...), custom_call_target="tpu_custom_call" | custom-call | tf_op jit(solution)/shard_map/propagate_later/pallas_call | solution.py:51
  57.3 15.5 %all_to_all.22.offset = f32[64,4,128]{2,1,0:T(4,128)S(1)} all-to-all(f32[64,4,128]{2,1,0:T(4,128)S(1)} %bitcast.16), channel_id=1, replica_groups=mesh['tm'=64,'sx'=2,'sy'=2] {'tm'}, dimensions={0} | all-to-all | bytes 262144 | tf_op jit(solution)/shard_map/all_to_all | solution.py:467
  72.7 0.7 cycle_later.1
  73.4 15.2 %all_to_all.23 = f32[64,4,128]{2,1,0:T(4,128)S(1)} all-to-all(f32[64,4,128]{2,1,0:T(4,128)S(1)} %get-tuple-element.36), channel_id=1, replica_groups=mesh['tm'=64,'sx'=2,'sy'=2] {'tm'}, dimensions={0} | all-to-all | bytes 262144 | tf_op jit(solution)/shard_map/all_to_all | solution.py:477
  88.6 0.7 copy.11
  (1 shorter events, 0.0 us)
Async XLA Ops:
  0.6 2.0 %collective-permute-start = (f32[256,128]{1,0:T(8,128)}, f32[256,128]{1,0:T(8,128)S(1)}, u32[]{:S(2)}, u32[]{:S(2)}) collective-permute-start(f32[256,128]{1,0:T(8,128)} %bitcast.20), channel_id=1, source_target_pairs={{0,2},{2,0},{1,3},{3,1},{4,6},{6,4},{5,7},{7,5},{8,10},{10,8},{9,1... | collective-permute-start | bytes 393224 | tf_op jit(solution)/shard_map/ppermute | solution.py:423
  0.7 1.9 %collective-permute-start.1 = (f32[256,128]{1,0:T(8,128)}, f32[256,128]{1,0:T(8,128)S(1)}, u32[]{:S(2)}, u32[]{:S(2)}) collective-permute-start(f32[256,128]{1,0:T(8,128)} %bitcast.22), channel_id=1, source_target_pairs={{0,2},{2,0},{1,3},{3,1},{4,6},{6,4},{5,7},{7,5},{8,10},{10,8},{9,1... | collective-permute-start | bytes 393224 | tf_op jit(solution)/shard_map/ppermute | solution.py:424
  2.6 2.4 %copy-start = (s32[8,8]{1,0:T(8,128)S(1)}, s32[8,8]{1,0:T(8,128)}, u32[]{:S(2)}) copy-start(s32[8,8]{1,0:T(8,128)} %ids.1) | copy-start | bytes 772
  2.6 2.4 %copy-start.1 = (s32[1,4,8]{2,1,0:T(4,128)S(1)}, s32[1,4,8]{2,1,0:T(4,128)}, u32[]{:S(2)}) copy-start(s32[1,4,8]{2,1,0:T(4,128)} %param.9) | copy-start | bytes 388
  2.9 2.2 %copy-start.2 = (f32[4]{0:T(128)S(1)}, f32[4]{0:T(128)}, u32[]{:S(2)}) copy-start(f32[4]{0:T(128)} %conductivity.1) | copy-start | bytes 52
  2.9 6.3 %collective-permute-start.2 = (f32[22,8,128]{2,1,0:T(8,128)S(1)}, f32[22,8,128]{2,1,0:T(8,128)S(1)}, u32[]{:S(2)}, u32[]{:S(2)}) collective-permute-start(f32[22,8,128]{2,1,0:T(8,128)S(1)} %pack.1), channel_id=1, source_target_pairs={{0,1},{1,0},{2,3},{3,2},{4,5},{5,4},{6,7},{7,6},{8,9},{9,8},{10,11... | collective-permute-start | bytes 270344 | tf_op jit(solution)/shard_map/ppermute | solution.py:436
  53.0 1.4 %collective-permute-start.3 = (f32[20,8,128]{2,1,0:T(8,128)S(1)}, f32[20,8,128]{2,1,0:T(8,128)S(1)}, u32[]{:S(2)}, u32[]{:S(2)}) collective-permute-start(f32[20,8,128]{2,1,0:T(8,128)S(1)} %get-tuple-element.30), channel_id=1, source_target_pairs={{0,2},{2,0},{1,3},{3,1},{4,6},{6,4},{5,7},{7,5},{8,10},{10,8},{9,1... | collective-permute-start | bytes 245768 | tf_op jit(solution)/shard_map/ppermute | solution.py:458

commit v8 on v7

--- a/solution.py
+++ b/solution.py
@@ -339,9 +339,11 @@
     left = here[1] == 0
     shift = fringe_shift(left)
     fringe = (slot >= shift) & (slot < shift + HALO)
+    def at_start(r):
+        return own[r] if r < ROWS else far[BOX - 1 - r]
+
     for r in range(BOX):
-        row = own[r] if r < ROWS else far[BOX - 1 - r]
-        tile[0][0, r] = row
+        tile[0][0, r] = at_start(r)
     for i in range(PACK):
         parts = []
         for g in range(2):
@@ -349,7 +351,7 @@
             source, k, at = (own, r, ROWS) if r < ROWS else (far, 2 * ROWS - 1 - r, HALO)
             parts.append(moved(source[at + k % FRINGE], g * WIDE - 32 * (k // FRINGE), shift))
         beside = jnp.where(lane < WIDE, parts[0], parts[1])
-        row = jnp.where(fringe, beside, banded(i, lambda r: tile[0][0, r]))
+        row = jnp.where(fringe, beside, banded(i, at_start))
         band[0][0, i] = row
     advance(
         tile_part(base, heat, power, tile),

time: 89.5 us -> 89.5 us (level)
  no operation moved by 1% of the time
where the time goes in v8:
time: 89.5 us; the launch traced here: 89.3 us
  blocking collectives  72 us (80%)
  Pallas kernels  10.2 us (11%)
  waiting for transfers between devices  2.85 us (3%)
  starting transfers between devices  2.84 us (3%)
    all_to_all x2, blocking collectives, spread(): return lax.all_to_all(x, 'tm', 0, 0, tiled=True).reshape(-1, COLS)  41.3 us
    all_to_all x1, blocking collectives, shards(): lax.all_to_all(later.reshape(slabs, 4, COLS), 'tm', 0, 0, tiled=True)  15.5 us
    all_to_all x1, blocking collectives, shards(): states = lax.all_to_all(states, 'tm', 0, 0, tiled=True)  15.2 us
    pallas_call x7, Pallas kernels, call(): pl.pallas_call(kernel, out_shape=outs, in_specs=[sspec()] * len(scalars)...  9.51 us
    ppermute x1, starting transfers between devices, shards(): other = lax.ppermute(sent, 'sy', SWAP)  2.16 us
  transfers between devices with their start and end apart: 4, of which 2 were waited for; matrix products, arithmetic and copies ran while one was open for 0% of the time, Pallas kernels for 4%

profile of v8, /device:TPU:16, one launch (start us, length us, event | category | flops | bytes accessed | tf_op | source)
XLA Modules:
  0.0 89.3 jit_solution(3483974551439352747)
XLA Ops:
  0.6 0.1 collective-permute-start
  0.7 0.5 collective-permute-start.1
  1.2 1.3 %load.1 = (f32[32,8,128]{2,1,0:T(8,128)S(1)}, f32[32,8,128]{2,1,0:T(8,128)S(1)}, f32[32,8,128]{2,1,0:T(8,128)S(1)}) custom-call(f32[256,128]{1,0:T(8,128)} %bitcast.21, f32[256,128]{1,0:T(8,128)} %bitcast.23, f32[256,128]{1,0:T(8,128)} %bitcast.19), custom_call_target="tpu_custom_call" | custom-call | flops 2000000 | bytes 800000 | tf_op jit(solution)/shard_map/load/pallas_call | solution.py:51
  2.6 0.0 collective-permute-done.far
  2.6 0.0 collective-permute-done.1.power_far
  2.6 0.0 copy-start
  2.6 0.0 copy-start.1
  2.6 0.2 pack.1
  2.9 0.0 copy-start.2
  2.9 2.2 %collective-permute-start.2 = (f32[22,8,128]{2,1,0:T(8,128)S(1)}, f32[22,8,128]{2,1,0:T(8,128)S(1)}, u32[]{:S(2)}, u32[]{:S(2)}) collective-permute-start(f32[22,8,128]{2,1,0:T(8,128)S(1)} %pack.1), channel_id=1, source_target_pairs={{0,1},{1,0},{2,3},{3,2},{4,5},{5,4},{6,7},{7,6},{8,9},{9,8},{10,11... | collective-permute-start | bytes 270344 | tf_op jit(solution)/shard_map/ppermute | solution.py:438
  5.0 0.0 copy-done
  5.0 0.0 copy-done.1
  5.0 0.0 copy-done.2
  5.0 2.5 %propagate_tile.1 = (f32[32,8,128]{2,1,0:T(8,128)S(1)}, f32[6,8,128]{2,1,0:T(8,128)S(1)}, f32[24,8,128]{2,1,0:T(8,128)S(1)}, f32[44,8,128]{2,1,0:T(8,128)S(1)}, ...) custom-call(s32[4,8]{1,0:T(4,128)S(1)} %bitcast.17, s32[8,8]{1,0:T(8,128)S(1)} %copy-done, f32[4]{0:T(128)S(1)} %copy-done.2, ...), custom_call_target="tpu_custom_call" | custom-call | flops 20000000 | bytes 4000000 | tf_op jit(solution)/shard_map/propagate_tile/pallas_call | solution.py:51
  7.6 1.6 %collective-permute-done.2.other = f32[22,8,128]{2,1,0:T(8,128)S(1)} collective-permute-done((f32[22,8,128]{2,1,0:T(8,128)S(1)}, f32[22,8,128]{2,1,0:T(8,128)S(1)}, u32[]{:S(2)}, u32[]{:S(2)}) %collective-permute-start.2) | collective-permute-done | bytes 90144 | tf_op jit(solution)/shard_map/ppermute | solution.py:438
  9.2 2.1 %propagate_band.1 = (f32[22,8,128]{2,1,0:T(8,128)S(1)}, f32[32,8,128]{2,1,0:T(8,128)S(1)}, f32[576,128]{1,0:T(8,128)S(1)}) custom-call(f32[32,8,128]{2,1,0:T(8,128)S(1)} %get-tuple-element.22.end, f32[32,8,128]{2,1,0:T(8,128)S(1)} %get-tuple-element.20.own.start, f32[32,8,128]{2,1,0:T(8,128)S(1)} %get-tuple-element.23.rate, ...), custom_call_target="tpu_custom_call" | custom-call | tf_op jit(solution)/shard_map/propagate_band/pallas_call | solution.py:51
  11.3 24.7 %all_to_all.20 = f32[64,9,1,128]{3,2,1,0:T(1,128)S(1)} all-to-all(f32[64,9,1,128]{3,2,1,0:T(1,128)S(1)} %bitcast.15), channel_id=1, replica_groups=mesh['tm'=64,'sx'=2,'sy'=2] {'tm'}, dimensions={0} | all-to-all | bytes 589824 | tf_op jit(solution)/shard_map/all_to_all | solution.py:415
  36.0 0.3 cycle.1
  36.3 16.6 %all_to_all.21 = f32[64,5,1,128]{3,2,1,0:T(1,128)S(1)} all-to-all(f32[64,5,1,128]{3,2,1,0:T(1,128)S(1)} %bitcast.13), channel_id=1, replica_groups=mesh['tm'=64,'sx'=2,'sy'=2] {'tm'}, dimensions={0} | all-to-all | bytes 327680 | tf_op jit(solution)/shard_map/all_to_all | solution.py:415
  53.0 0.1 collective-permute-start.3
  53.1 1.3 %collective-permute-done.3.far = f32[20,8,128]{2,1,0:T(8,128)S(1)} collective-permute-done((f32[20,8,128]{2,1,0:T(8,128)S(1)}, f32[20,8,128]{2,1,0:T(8,128)S(1)}, u32[]{:S(2)}, u32[]{:S(2)}) %collective-permute-start.3) | collective-permute-done | bytes 81952 | tf_op jit(solution)/shard_map/ppermute | solution.py:460
  54.3 2.9 %propagate_later.1 = (f32[256,128]{1,0:T(8,128)S(1)}, f32[256,128]{1,0:T(8,128)S(1)}) custom-call(f32[40,8,128]{2,1,0:T(8,128)S(1)} %get-tuple-element.29.own, f32[20,8,128]{2,1,0:T(8,128)S(1)} %collective-permute-done.3.far, f32[32,8,128]{2,1,0:T(8,128)S(1)} %get-tuple-element.23.rate, f32[6,8,128]{2,1,0:T(8,128)S(1)} %get-tuple-element.24.base, ...), custom_call_target="tpu_custom_call" | custom-call | tf_op jit(solution)/shard_map/propagate_later/pallas_call | solution.py:51
  57.3 15.5 %all_to_all.22.offset = f32[64,4,128]{2,1,0:T(4,128)S(1)} all-to-all(f32[64,4,128]{2,1,0:T(4,128)S(1)} %bitcast.16), channel_id=1, replica_groups=mesh['tm'=64,'sx'=2,'sy'=2] {'tm'}, dimensions={0} | all-to-all | bytes 262144 | tf_op jit(solution)/shard_map/all_to_all | solution.py:469
  72.7 0.7 cycle_later.1
  73.4 15.2 %all_to_all.23 = f32[64,4,128]{2,1,0:T(4,128)S(1)} all-to-all(f32[64,4,128]{2,1,0:T(4,128)S(1)} %get-tuple-element.36), channel_id=1, replica_groups=mesh['tm'=64,'sx'=2,'sy'=2] {'tm'}, dimensions={0} | all-to-all | bytes 262144 | tf_op jit(solution)/shard_map/all_to_all | solution.py:479
  88.6 0.7 copy.11
  (1 shorter events, 0.0 us)
Async XLA Ops:
  0.6 2.0 %collective-permute-start = (f32[256,128]{1,0:T(8,128)}, f32[256,128]{1,0:T(8,128)S(1)}, u32[]{:S(2)}, u32[]{:S(2)}) collective-permute-start(f32[256,128]{1,0:T(8,128)} %bitcast.20), channel_id=1, source_target_pairs={{0,2},{2,0},{1,3},{3,1},{4,6},{6,4},{5,7},{7,5},{8,10},{10,8},{9,1... | collective-permute-start | bytes 393224 | tf_op jit(solution)/shard_map/ppermute | solution.py:425
  0.7 1.9 %collective-permute-start.1 = (f32[256,128]{1,0:T(8,128)}, f32[256,128]{1,0:T(8,128)S(1)}, u32[]{:S(2)}, u32[]{:S(2)}) collective-permute-start(f32[256,128]{1,0:T(8,128)} %bitcast.22), channel_id=1, source_target_pairs={{0,2},{2,0},{1,3},{3,1},{4,6},{6,4},{5,7},{7,5},{8,10},{10,8},{9,1... | collective-permute-start | bytes 393224 | tf_op jit(solution)/shard_map/ppermute | solution.py:426
  2.6 2.4 %copy-start = (s32[8,8]{1,0:T(8,128)S(1)}, s32[8,8]{1,0:T(8,128)}, u32[]{:S(2)}) copy-start(s32[8,8]{1,0:T(8,128)} %ids.1) | copy-start | bytes 772
  2.6 2.4 %copy-start.1 = (s32[1,4,8]{2,1,0:T(4,128)S(1)}, s32[1,4,8]{2,1,0:T(4,128)}, u32[]{:S(2)}) copy-start(s32[1,4,8]{2,1,0:T(4,128)} %param.9) | copy-start | bytes 388
  2.9 2.2 %copy-start.2 = (f32[4]{0:T(128)S(1)}, f32[4]{0:T(128)}, u32[]{:S(2)}) copy-start(f32[4]{0:T(128)} %conductivity.1) | copy-start | bytes 52
  2.9 6.3 %collective-permute-start.2 = (f32[22,8,128]{2,1,0:T(8,128)S(1)}, f32[22,8,128]{2,1,0:T(8,128)S(1)}, u32[]{:S(2)}, u32[]{:S(2)}) collective-permute-start(f32[22,8,128]{2,1,0:T(8,128)S(1)} %pack.1), channel_id=1, source_target_pairs={{0,1},{1,0},{2,3},{3,2},{4,5},{5,4},{6,7},{7,6},{8,9},{9,8},{10,11... | collective-permute-start | bytes 270344 | tf_op jit(solution)/shard_map/ppermute | solution.py:438
  53.0 1.4 %collective-permute-start.3 = (f32[20,8,128]{2,1,0:T(8,128)S(1)}, f32[20,8,128]{2,1,0:T(8,128)S(1)}, u32[]{:S(2)}, u32[]{:S(2)}) collective-permute-start(f32[20,8,128]{2,1,0:T(8,128)S(1)} %get-tuple-element.30), channel_id=1, source_target_pairs={{0,2},{2,0},{1,3},{3,1},{4,6},{6,4},{5,7},{7,5},{8,10},{10,8},{9,1... | collective-permute-start | bytes 245768 | tf_op jit(solution)/shard_map/ppermute | solution.py:460

commit v9 on v7

--- a/solution.py
+++ b/solution.py
@@ -122,6 +122,7 @@
         lane = lanes()
         layer = layers()
         edge = jnp.where(layer == 0, 1.0, 0.0)
+        share = jnp.where(layer == LAYERS - 1, 0.0, 0.5)
         if not packed:
             edge = edge + jnp.where(lane == 0, 1.0, 0.0) + jnp.where(lane == COLS - 1, 1.0, 0.0)
         cond = []
@@ -145,7 +146,7 @@
             north = c + moved(c, -1)
             if not packed:
                 north = jnp.where(lane == COLS - 1, 0.0, north)
-            up = jnp.where(layer == LAYERS - 1, 0.0, 0.5 * (c + pltpu.roll(c, LAYERS - 1, 0)))
+            up = share * (c + pltpu.roll(c, LAYERS - 1, 0))
             total = (north + moved(north, 1)) + (up + pltpu.roll(up, 1, 0)) + (1.0 + edge * c)
             low = faces[r]
             if r == 0:

time: 89.5 us -> 89.5 us (level)
  no operation moved by 1% of the time
where the time goes in v9:
time: 89.5 us; the launch traced here: 89.2 us
  blocking collectives  72 us (80%)
  Pallas kernels  10.2 us (11%)
  waiting for transfers between devices  2.85 us (3%)
  starting transfers between devices  2.84 us (3%)
    all_to_all x2, blocking collectives, spread(): return lax.all_to_all(x, 'tm', 0, 0, tiled=True).reshape(-1, COLS)  41.3 us
    all_to_all x1, blocking collectives, shards(): lax.all_to_all(later.reshape(slabs, 4, COLS), 'tm', 0, 0, tiled=True)  15.5 us
    all_to_all x1, blocking collectives, shards(): states = lax.all_to_all(states, 'tm', 0, 0, tiled=True)  15.2 us
    pallas_call x7, Pallas kernels, call(): pl.pallas_call(kernel, out_shape=outs, in_specs=[sspec()] * len(scalars)...  9.51 us
    ppermute x1, starting transfers between devices, shards(): other = lax.ppermute(sent, 'sy', SWAP)  2.16 us
  transfers between devices with their start and end apart: 4, of which 2 were waited for; matrix products, arithmetic and copies ran while one was open for 0% of the time, Pallas kernels for 4%

profile of v9, /device:TPU:16, one launch (start us, length us, event | category | flops | bytes accessed | tf_op | source)
XLA Modules:
  0.0 89.2 jit_solution(9443843056079841458)
XLA Ops:
  0.6 0.1 collective-permute-start
  0.7 0.5 collective-permute-start.1
  1.2 1.3 %load.1 = (f32[32,8,128]{2,1,0:T(8,128)S(1)}, f32[32,8,128]{2,1,0:T(8,128)S(1)}, f32[32,8,128]{2,1,0:T(8,128)S(1)}) custom-call(f32[256,128]{1,0:T(8,128)} %bitcast.21, f32[256,128]{1,0:T(8,128)} %bitcast.23, f32[256,128]{1,0:T(8,128)} %bitcast.19), custom_call_target="tpu_custom_call" | custom-call | flops 2000000 | bytes 800000 | tf_op jit(solution)/shard_map/load/pallas_call | solution.py:51
  2.6 0.0 collective-permute-done.far
  2.6 0.0 collective-permute-done.1.power_far
  2.6 0.0 copy-start
  2.6 0.0 copy-start.1
  2.6 0.2 pack.1
  2.9 0.0 copy-start.2
  2.9 2.2 %collective-permute-start.2 = (f32[22,8,128]{2,1,0:T(8,128)S(1)}, f32[22,8,128]{2,1,0:T(8,128)S(1)}, u32[]{:S(2)}, u32[]{:S(2)}) collective-permute-start(f32[22,8,128]{2,1,0:T(8,128)S(1)} %pack.1), channel_id=1, source_target_pairs={{0,1},{1,0},{2,3},{3,2},{4,5},{5,4},{6,7},{7,6},{8,9},{9,8},{10,11... | collective-permute-start | bytes 270344 | tf_op jit(solution)/shard_map/ppermute | solution.py:437
  5.0 0.0 copy-done
  5.0 0.0 copy-done.1
  5.0 0.0 copy-done.2
  5.0 2.5 %propagate_tile.1 = (f32[32,8,128]{2,1,0:T(8,128)S(1)}, f32[6,8,128]{2,1,0:T(8,128)S(1)}, f32[24,8,128]{2,1,0:T(8,128)S(1)}, f32[44,8,128]{2,1,0:T(8,128)S(1)}, ...) custom-call(s32[4,8]{1,0:T(4,128)S(1)} %bitcast.17, s32[8,8]{1,0:T(8,128)S(1)} %copy-done, f32[4]{0:T(128)S(1)} %copy-done.2, ...), custom_call_target="tpu_custom_call" | custom-call | flops 20000000 | bytes 4000000 | tf_op jit(solution)/shard_map/propagate_tile/pallas_call | solution.py:51
  7.6 1.6 %collective-permute-done.2.other = f32[22,8,128]{2,1,0:T(8,128)S(1)} collective-permute-done((f32[22,8,128]{2,1,0:T(8,128)S(1)}, f32[22,8,128]{2,1,0:T(8,128)S(1)}, u32[]{:S(2)}, u32[]{:S(2)}) %collective-permute-start.2) | collective-permute-done | bytes 90144 | tf_op jit(solution)/shard_map/ppermute | solution.py:437
  9.2 2.1 %propagate_band.1 = (f32[22,8,128]{2,1,0:T(8,128)S(1)}, f32[32,8,128]{2,1,0:T(8,128)S(1)}, f32[576,128]{1,0:T(8,128)S(1)}) custom-call(f32[32,8,128]{2,1,0:T(8,128)S(1)} %get-tuple-element.22.end, f32[32,8,128]{2,1,0:T(8,128)S(1)} %get-tuple-element.20.own.start, f32[32,8,128]{2,1,0:T(8,128)S(1)} %get-tuple-element.23.rate, ...), custom_call_target="tpu_custom_call" | custom-call | tf_op jit(solution)/shard_map/propagate_band/pallas_call | solution.py:51
  11.3 24.7 %all_to_all.20 = f32[64,9,1,128]{3,2,1,0:T(1,128)S(1)} all-to-all(f32[64,9,1,128]{3,2,1,0:T(1,128)S(1)} %bitcast.15), channel_id=1, replica_groups=mesh['tm'=64,'sx'=2,'sy'=2] {'tm'}, dimensions={0} | all-to-all | bytes 589824 | tf_op jit(solution)/shard_map/all_to_all | solution.py:414
  36.0 0.3 cycle.1
  36.3 16.6 %all_to_all.21 = f32[64,5,1,128]{3,2,1,0:T(1,128)S(1)} all-to-all(f32[64,5,1,128]{3,2,1,0:T(1,128)S(1)} %bitcast.13), channel_id=1, replica_groups=mesh['tm'=64,'sx'=2,'sy'=2] {'tm'}, dimensions={0} | all-to-all | bytes 327680 | tf_op jit(solution)/shard_map/all_to_all | solution.py:414
  53.0 0.1 collective-permute-start.3
  53.1 1.3 %collective-permute-done.3.far = f32[20,8,128]{2,1,0:T(8,128)S(1)} collective-permute-done((f32[20,8,128]{2,1,0:T(8,128)S(1)}, f32[20,8,128]{2,1,0:T(8,128)S(1)}, u32[]{:S(2)}, u32[]{:S(2)}) %collective-permute-start.3) | collective-permute-done | bytes 81952 | tf_op jit(solution)/shard_map/ppermute | solution.py:459
  54.3 2.9 %propagate_later.1 = (f32[256,128]{1,0:T(8,128)S(1)}, f32[256,128]{1,0:T(8,128)S(1)}) custom-call(f32[40,8,128]{2,1,0:T(8,128)S(1)} %get-tuple-element.29.own, f32[20,8,128]{2,1,0:T(8,128)S(1)} %collective-permute-done.3.far, f32[32,8,128]{2,1,0:T(8,128)S(1)} %get-tuple-element.23.rate, f32[6,8,128]{2,1,0:T(8,128)S(1)} %get-tuple-element.24.base, ...), custom_call_target="tpu_custom_call" | custom-call | tf_op jit(solution)/shard_map/propagate_later/pallas_call | solution.py:51
  57.3 15.5 %all_to_all.22.offset = f32[64,4,128]{2,1,0:T(4,128)S(1)} all-to-all(f32[64,4,128]{2,1,0:T(4,128)S(1)} %bitcast.16), channel_id=1, replica_groups=mesh['tm'=64,'sx'=2,'sy'=2] {'tm'}, dimensions={0} | all-to-all | bytes 262144 | tf_op jit(solution)/shard_map/all_to_all | solution.py:468
  72.7 0.7 cycle_later.1
  73.4 15.2 %all_to_all.23 = f32[64,4,128]{2,1,0:T(4,128)S(1)} all-to-all(f32[64,4,128]{2,1,0:T(4,128)S(1)} %get-tuple-element.36), channel_id=1, replica_groups=mesh['tm'=64,'sx'=2,'sy'=2] {'tm'}, dimensions={0} | all-to-all | bytes 262144 | tf_op jit(solution)/shard_map/all_to_all | solution.py:478
  88.6 0.7 copy.11
  (1 shorter events, 0.0 us)
Async XLA Ops:
  0.6 2.0 %collective-permute-start = (f32[256,128]{1,0:T(8,128)}, f32[256,128]{1,0:T(8,128)S(1)}, u32[]{:S(2)}, u32[]{:S(2)}) collective-permute-start(f32[256,128]{1,0:T(8,128)} %bitcast.20), channel_id=1, source_target_pairs={{0,2},{2,0},{1,3},{3,1},{4,6},{6,4},{5,7},{7,5},{8,10},{10,8},{9,1... | collective-permute-start | bytes 393224 | tf_op jit(solution)/shard_map/ppermute | solution.py:424
  0.7 1.9 %collective-permute-start.1 = (f32[256,128]{1,0:T(8,128)}, f32[256,128]{1,0:T(8,128)S(1)}, u32[]{:S(2)}, u32[]{:S(2)}) collective-permute-start(f32[256,128]{1,0:T(8,128)} %bitcast.22), channel_id=1, source_target_pairs={{0,2},{2,0},{1,3},{3,1},{4,6},{6,4},{5,7},{7,5},{8,10},{10,8},{9,1... | collective-permute-start | bytes 393224 | tf_op jit(solution)/shard_map/ppermute | solution.py:425
  2.6 2.4 %copy-start = (s32[8,8]{1,0:T(8,128)S(1)}, s32[8,8]{1,0:T(8,128)}, u32[]{:S(2)}) copy-start(s32[8,8]{1,0:T(8,128)} %ids.1) | copy-start | bytes 772
  2.6 2.4 %copy-start.1 = (s32[1,4,8]{2,1,0:T(4,128)S(1)}, s32[1,4,8]{2,1,0:T(4,128)}, u32[]{:S(2)}) copy-start(s32[1,4,8]{2,1,0:T(4,128)} %param.9) | copy-start | bytes 388
  2.9 2.2 %copy-start.2 = (f32[4]{0:T(128)S(1)}, f32[4]{0:T(128)}, u32[]{:S(2)}) copy-start(f32[4]{0:T(128)} %conductivity.1) | copy-start | bytes 52
  2.9 6.3 %collective-permute-start.2 = (f32[22,8,128]{2,1,0:T(8,128)S(1)}, f32[22,8,128]{2,1,0:T(8,128)S(1)}, u32[]{:S(2)}, u32[]{:S(2)}) collective-permute-start(f32[22,8,128]{2,1,0:T(8,128)S(1)} %pack.1), channel_id=1, source_target_pairs={{0,1},{1,0},{2,3},{3,2},{4,5},{5,4},{6,7},{7,6},{8,9},{9,8},{10,11... | collective-permute-start | bytes 270344 | tf_op jit(solution)/shard_map/ppermute | solution.py:437
  53.0 1.4 %collective-permute-start.3 = (f32[20,8,128]{2,1,0:T(8,128)S(1)}, f32[20,8,128]{2,1,0:T(8,128)S(1)}, u32[]{:S(2)}, u32[]{:S(2)}) collective-permute-start(f32[20,8,128]{2,1,0:T(8,128)S(1)} %get-tuple-element.30), channel_id=1, source_target_pairs={{0,2},{2,0},{1,3},{3,1},{4,6},{6,4},{5,7},{7,5},{8,10},{10,8},{9,1... | collective-permute-start | bytes 245768 | tf_op jit(solution)/shard_map/ppermute | solution.py:459
